TPU v7x, 32 devices: a whole 2x2x4 slice. The times are simulated.
32 devices in a mesh: dp: 4 (over z), head: 4 (over x, core), group: 2 (over y).
Axes of the slice: x: 2, y: 2, z: 4, core: 2. Of those that a mesh axis runs over, the one named last changes fastest.
Arguments:
- tokens: bfloat16 [2048, 2048], P(('dp', 'head')), may hold values from -6 to 6
- grad_out: bfloat16 [2048, 2048], P(('dp', 'head')), may hold values from -6 to 6
- w_qkv: bfloat16 [3, 2048, 1024], P(None, None, ('head', 'group')), may hold values from -4 to 4
- w_attn_out: bfloat16 [1024, 2048], P(('head', 'group')), may hold values from -0.1875 to 0.1875
- gain_attn: float32 [2048], replicated, may hold values from 0.25 to 1.75
- gain_ffn: float32 [2048], replicated, may hold values from 0.25 to 1.75
- w_gate_up: bfloat16 [16, 2, 2048, 1408], P(('dp', 'head'), None, None, 'group'), may hold values from -0.125 to 0.125
- w_down: bfloat16 [16, 1408, 2048], P(('dp', 'head'), 'group'), may hold values from -0.15625 to 0.15625
- expert_ids: int32 [2048, 2], P(('dp', 'head')), may hold values from 0 to 15, all different within a row; in each aligned block of 128 rows (0 to 127, 128 to 255, ...) at most 20 rows name the same one
- gates: float32 [2048, 2], P(('dp', 'head')), may hold values from 0.05 to 0.5
Outputs:
- grad_tokens: bfloat16 [2048, 2048], P(('dp', 'head'))
- grad_qkv: float32 [3, 2048, 1024], P(None, 'dp', ('head', 'group'))
- grad_attn_out: float32 [1024, 2048], P(('head', 'group'), 'dp')
- grad_gate_up: bfloat16 [16, 2, 2048, 1408], P(('dp', 'head'), None, None, 'group')
- grad_down: bfloat16 [16, 1408, 2048], P(('dp', 'head'), 'group')
Inputs may be any that keep to these rules, and one draw needn't show every extreme that they name: `expert_ids`: each row names 2 different experts; in each aligned block of 128 rows no expert is named by more than 20 rows.
All inputs are finite; a program needn't handle non-finite values.
Results may differ from a plain program's by a relative error of at most 0.012.
Values may be sent and summed in bfloat16 or wider, within the bound.
A program may use at most 128 MiB of HBM per device.

v0:
```python
import jax
import jax.numpy as jnp
from jax import lax
from jax.sharding import PartitionSpec as P

HD = 128


epsilon = 1e-06


def inverse_rms(values):
    return lax.rsqrt(jnp.mean(values * values, axis=-1, keepdims=True) + epsilon)


def norm_backward(values, scaling, gain, upstream):
    weighted = upstream * gain
    normed = values * scaling
    return scaling * (weighted - normed * jnp.mean(weighted * normed, axis=-1, keepdims=True))


def attention_probs(query_heads, key_heads):
    length = query_heads.shape[0]
    scores = jnp.einsum(
        "qhd,khd->hqk", query_heads, key_heads, preferred_element_type=jnp.float32
    ) * HD ** (-0.5)
    row_pos = lax.broadcasted_iota(jnp.int32, (length, length), 0)
    col_pos = lax.broadcasted_iota(jnp.int32, (length, length), 1)
    scores = jnp.where((col_pos <= row_pos)[None], scores, -1e30)
    maxima = jnp.max(scores, axis=-1, keepdims=True)
    powered = jnp.exp(scores - maxima)
    return powered / jnp.sum(powered, axis=-1, keepdims=True)


def expert_work(in_rows, in_grads, w_gate_up, w_down):
    gate_w = w_gate_up[:, 0]
    up_w = w_gate_up[:, 1]
    gate_pre = jnp.einsum("esd,edf->esf", in_rows, gate_w, preferred_element_type=jnp.float32)
    up_pre = jnp.einsum("esd,edf->esf", in_rows, up_w, preferred_element_type=jnp.float32)
    sigma = jax.nn.sigmoid(gate_pre)
    active = gate_pre * sigma
    product = (active * up_pre).astype(jnp.bfloat16)
    upstream = jnp.einsum("esd,efd->esf", in_grads, w_down, preferred_element_type=jnp.float32)
    grad_down = jnp.einsum(
        "esf,esd->efd", product, in_grads, preferred_element_type=jnp.float32
    ).astype(jnp.bfloat16)
    grad_gate = (upstream * up_pre * sigma * (1.0 + gate_pre * (1.0 - sigma))).astype(jnp.bfloat16)
    grad_up = (upstream * active).astype(jnp.bfloat16)
    grad_pair = jnp.stack(
        [
            jnp.einsum("esd,esf->edf", in_rows, grad_gate, preferred_element_type=jnp.float32),
            jnp.einsum("esd,esf->edf", in_rows, grad_up, preferred_element_type=jnp.float32),
        ],
        axis=1,
    ).astype(jnp.bfloat16)
    returned = jnp.einsum("esf,edf->esd", grad_gate, gate_w, preferred_element_type=jnp.float32)
    returned = returned + jnp.einsum(
        "esf,edf->esd", grad_up, up_w, preferred_element_type=jnp.float32
    )
    return (grad_pair, grad_down, returned)


def body(
    tokens, grad_out, w_qkv, w_attn_out, gain_attn, gain_ffn, w_gate_up, w_down, expert_ids, gates
):
    row_count, width = tokens.shape
    seq_len = row_count * lax.axis_size("head")
    head_cols = w_qkv.shape[2]
    head_count = head_cols // HD
    tokens_f = tokens.astype(jnp.float32)
    scale_one = inverse_rms(tokens_f)
    normed_one = (tokens_f * scale_one * gain_attn).astype(jnp.bfloat16)
    shard_rows = lax.all_gather(normed_one, "head", axis=0, tiled=True)
    fresh = jnp.einsum("rd,idh->irh", shard_rows, w_qkv, preferred_element_type=jnp.float32).astype(
        jnp.bfloat16
    )
    projected = fresh
    gathered = shard_rows
    projected, normed_all = (projected, gathered)
    split_heads = projected.reshape(3, seq_len, head_count, HD)
    query_heads = split_heads[0]
    key_heads = split_heads[1]
    value_heads = split_heads[2]
    chances = attention_probs(query_heads, key_heads)
    weights_b = chances.astype(jnp.bfloat16)
    mixed = (
        jnp.einsum("hqk,khd->qhd", weights_b, value_heads, preferred_element_type=jnp.float32)
        .astype(jnp.bfloat16)
        .reshape(seq_len, head_cols)
    )
    attn_part = lax.psum_scatter(
        jnp.dot(mixed, w_attn_out, preferred_element_type=jnp.float32),
        "head",
        scatter_dimension=0,
        tiled=True,
    )
    attn_sum = lax.psum(attn_part, "group")
    hidden = (tokens_f + attn_sum).astype(jnp.bfloat16)
    hidden_f = hidden.astype(jnp.float32)
    scale_two = inverse_rms(hidden_f)
    normed_two = (hidden_f * scale_two * gain_ffn).astype(jnp.bfloat16)
    grad_f = grad_out.astype(jnp.float32)
    top_count = expert_ids.shape[1]
    owners = lax.axis_size(("dp", "head"))
    local_count = w_gate_up.shape[0]
    expert_count = local_count * owners
    capacity = max(row_count * top_count * 5 // (4 * expert_count), 2)
    flat_ids = expert_ids.reshape(-1)
    onehot = (flat_ids[:, None] == lax.iota(jnp.int32, expert_count)[None, :]).astype(jnp.int32)
    earlier = jnp.cumsum(onehot, axis=0) - onehot
    slot_ids = jnp.sum(onehot * earlier, axis=1)
    targets = flat_ids * capacity + slot_ids
    matches = (lax.iota(jnp.int32, expert_count * capacity)[:, None] == targets[None, :]).reshape(
        expert_count * capacity, row_count, top_count
    )
    picker = jnp.any(matches, axis=2).astype(jnp.bfloat16)
    weigher = jnp.sum(jnp.where(matches, gates[None, :, :], 0.0), axis=2)
    send_rows = (
        jnp.dot(picker, normed_two, preferred_element_type=jnp.float32)
        .astype(jnp.bfloat16)
        .reshape(expert_count, capacity, width)
    )
    send_grads = (
        jnp.dot(
            weigher, grad_f, precision=lax.Precision.HIGHEST, preferred_element_type=jnp.float32
        )
        .astype(jnp.bfloat16)
        .reshape(expert_count, capacity, width)
    )
    got_rows, got_grads = (
        lax.all_to_all(send_rows, ("dp", "head"), split_axis=0, concat_axis=1, tiled=True),
        lax.all_to_all(send_grads, ("dp", "head"), split_axis=0, concat_axis=1, tiled=True),
    )
    grad_pair, grad_down, returned = expert_work(got_rows, got_grads, w_gate_up, w_down)
    shared = lax.psum_scatter(returned, "group", scatter_dimension=2, tiled=True)
    back_half = lax.all_to_all(
        shared.astype(jnp.bfloat16), ("dp", "head"), split_axis=1, concat_axis=0, tiled=True
    )
    back_rows = lax.all_gather(back_half, "group", axis=2, tiled=True)
    grad_normed = jnp.einsum(
        "cr,cd->rd",
        picker,
        back_rows.reshape(expert_count * capacity, width),
        preferred_element_type=jnp.float32,
    )
    grad_hidden = grad_f + norm_backward(hidden_f, scale_two, gain_ffn, grad_normed)
    grad_hidden_b = grad_hidden.astype(jnp.bfloat16)
    shard_rows = lax.all_gather(grad_hidden_b, "head", axis=0, tiled=True)
    weight_total = jnp.einsum("rh,rd->hd", mixed, shard_rows, preferred_element_type=jnp.float32)
    fresh = jnp.einsum(
        "rd,hd->rh", shard_rows, w_attn_out, preferred_element_type=jnp.float32
    ).astype(jnp.bfloat16)
    grad_mixed = fresh
    grad_out_w, grad_mixed = (weight_total, grad_mixed)
    grad_heads = grad_mixed.reshape(seq_len, head_count, HD)
    grad_weights = jnp.einsum(
        "qhd,khd->hqk", grad_heads, value_heads, preferred_element_type=jnp.float32
    )
    grad_values = jnp.einsum(
        "hqk,qhd->khd", weights_b, grad_heads, preferred_element_type=jnp.float32
    ).astype(jnp.bfloat16)
    row_total = jnp.sum(chances * grad_weights, axis=-1, keepdims=True)
    grad_scores = (chances * (grad_weights - row_total) * HD ** (-0.5)).astype(jnp.bfloat16)
    grad_queries = jnp.einsum(
        "hqk,khd->qhd", grad_scores, key_heads, preferred_element_type=jnp.float32
    ).astype(jnp.bfloat16)
    grad_keys = jnp.einsum(
        "hqk,qhd->khd", grad_scores, query_heads, preferred_element_type=jnp.float32
    ).astype(jnp.bfloat16)
    grad_acts = jnp.stack([grad_queries, grad_keys, grad_values]).reshape(3, seq_len, head_cols)
    grad_proj = jnp.einsum("sd,ish->idh", normed_all, grad_acts, preferred_element_type=jnp.float32)
    input_part = lax.psum_scatter(
        jnp.einsum("irh,idh->rd", grad_acts, w_qkv, preferred_element_type=jnp.float32),
        "head",
        scatter_dimension=0,
        tiled=True,
    )
    grad_normed_one = lax.psum(input_part, "group")
    grad_proj_sum, grad_out_sum = (
        lax.psum_scatter(grad_proj, "dp", scatter_dimension=1, tiled=True),
        lax.psum_scatter(grad_out_w, "dp", scatter_dimension=1, tiled=True),
    )
    grad_tokens = (
        grad_hidden + norm_backward(tokens_f, scale_one, gain_attn, grad_normed_one)
    ).astype(jnp.bfloat16)
    return (grad_tokens, grad_proj_sum, grad_out_sum, grad_pair, grad_down)


def solution(mesh):
    return jax.shard_map(
        body,
        mesh=mesh,
        in_specs=(
            P(("dp", "head"), None),
            P(("dp", "head"), None),
            P(None, None, ("head", "group")),
            P(("head", "group"), None),
            P(),
            P(),
            P(("dp", "head"), None, None, "group"),
            P(("dp", "head"), "group", None),
            P(("dp", "head"), None),
            P(("dp", "head"), None),
        ),
        out_specs=(
            P(("dp", "head"), None),
            P(None, "dp", ("head", "group")),
            P(("head", "group"), "dp"),
            P(("dp", "head"), None, None, "group"),
            P(("dp", "head"), "group", None),
        ),
        check_vma=False,
    )
```

profile of v0, /device:TPU:0, one launch (start us, length us, event | category | flops | bytes accessed | tf_op | source)
XLA Modules:
  0.0 529.8 jit_solution(7929135334479818587)
XLA Ops:
  7.2 1.4 fusion.55
  8.6 2.0 fusion.49
  10.7 25.4 %all-gather.4.cloned.1.call-done = bf16[512,2048]{1,0:T(8,128)(2,1)} async-done(((bf16[128,2048]{1,0:T(8,128)(2,1)}), bf16[512,2048]{1,0:T(8,128)(2,1)}) %all-gather.4.cloned.1.call-update) | async-done | bytes 2097168 | tf_op jit(solution)/shard_map/all_gather | solution.py:73
  36.1 3.3 fusion.36
  41.8 2.7 fusion.80
  46.9 2.2 convolution_convert_fusion.4
  49.1 3.3 reshape.282
  52.4 4.8 all-to-all-start
  57.2 43.8 %reduce-scatter.6.cloned.1.call-done = f32[128,2048]{1,0:T(8,128)} async-done(((f32[512,2048]{1,0:T(8,128)}), f32[128,2048]{1,0:T(8,128)}) %reduce-scatter.6.cloned.1.call-update) | async-done | bytes 1048592 | tf_op jit(solution)/shard_map/reduce_scatter | solution.py:91
  101.1 42.4 %all-reduce.3.cloned.1.call-done = f32[128,2048]{1,0:T(8,128)} async-done(((f32[128,2048]{1,0:T(8,128)}), f32[128,2048]{1,0:T(8,128)}) %all-reduce.3.cloned.1.call-update) | async-done | bytes 1048592 | tf_op jit(solution)/shard_map/psum | solution.py:97
  143.4 1.5 fusion.48
  145.7 1.6 convolution_convert_fusion.3
  147.3 3.2 reshape.285
  150.5 5.7 %all-to-all-start.1 = ((bf16[16,20,2048]{2,1,0:T(8,128)(2,1)}), bf16[16,20,2048]{2,1,0:T(8,128)(2,1)}, u32[]{:S(2)}, u32[]{:S(2)}) async-start(bf16[16,20,2048]{2,1,0:T(8,128)(2,1)} %reshape.285), calls=%async_computation.2 | async-start | bytes 3145728 | tf_op jit(solution)/shard_map/all_to_all | solution.py:131
  156.4 3.3 reshape.283
  159.7 28.5 %all-to-all-done.1 = bf16[16,20,2048]{2,1,0:T(8,128)(2,1)} async-done(((bf16[16,20,2048]{2,1,0:T(8,128)(2,1)}), bf16[16,20,2048]{2,1,0:T(8,128)(2,1)}, u32[]{:S(2)}, u32[]{:S(2)}) %all-to-all-start.1) | async-done | bytes 1310752 | tf_op jit(solution)/shard_map/all_to_all | solution.py:131
  188.2 3.3 reshape.286
  191.5 3.5 fusion.5
  195.1 3.4 fusion.9
  198.6 1.6 multiply_convert_fusion.2
  200.4 1.2 fusion.3
  201.6 2.7 fusion.16
  204.4 41.2 %reduce-scatter.8.cloned.1.call-done = f32[1,320,1024]{2,1,0:T(8,128)} async-done(((f32[1,320,2048]{2,1,0:T(8,128)}), f32[1,320,1024]{2,1,0:T(8,128)}) %reduce-scatter.8.cloned.1.call-update) | async-done | bytes 1310736 | tf_op jit(solution)/shard_map/reduce_scatter | solution.py:135
  245.6 1.4 convert_element_type.139
  247.0 1.0 copy.57
  248.6 4.5 reduce.10
  253.5 23.6 %all_to_all.30 = bf16[16,2,10240]{2,1,0:T(2,128)(2,1)S(1)} all-to-all(bf16[16,2,10240]{2,1,0:T(2,128)(2,1)S(1)} %reshape.295), channel_id=1, replica_groups=mesh['dp'=4,'head'=4,'group'=2] {'dp','head'}, dimensions={0} | all-to-all | bytes 1310720 | tf_op jit(solution)/shard_map/all_to_all | solution.py:136
  277.8 3.8 bitcast_reduce_fusion
  282.7 25.0 %all-gather.6.cloned.1.call-done = bf16[16,20,2048]{2,1,0:T(8,128)(2,1)} async-done(((bf16[16,20,1024]{2,1,0:T(8,128)(2,1)}), bf16[16,20,2048]{2,1,0:T(8,128)(2,1)}) %all-gather.6.cloned.1.call-update) | async-done | bytes 1310736 | tf_op jit(solution)/shard_map/all_gather | solution.py:139
  307.6 2.3 reshape.289
  311.0 1.2 fusion.75
  312.2 22.7 %all-gather.8.cloned.1.call-done = bf16[512,2048]{1,0:T(8,128)(2,1)} async-done(((bf16[128,2048]{1,0:T(8,128)(2,1)}), bf16[512,2048]{1,0:T(8,128)(2,1)}) %all-gather.8.cloned.1.call-update) | async-done | bytes 2097168 | tf_op jit(solution)/shard_map/all_gather | solution.py:148
  334.9 2.3 convolution_convert_fusion.8
  340.0 3.3 convolution_bitcast_fusion
  343.4 1.5 copy-done.12
  344.9 2.6 convolution_bitcast_fusion.1
  347.6 40.4 %reduce-scatter.10.cloned.1.call-done = f32[128,2048]{1,0:T(8,128)} async-done(((f32[512,2048]{1,0:T(8,128)}), f32[128,2048]{1,0:T(8,128)}) %reduce-scatter.10.cloned.1.call-update) | async-done | bytes 1048592 | tf_op jit(solution)/shard_map/reduce_scatter | solution.py:172
  388.3 1.4 fusion.81
  389.8 3.3 fusion.1
  393.1 1.7 fusion
  394.9 3.1 pad_maximum_fusion
  398.1 3.3 fusion.2
  401.4 49.1 %reduce-scatter.12.cloned.1.call-done = f32[3,512,128]{1,2,0:T(8,128)} async-done(((f32[3,2048,128]{1,2,0:T(8,128)}), f32[3,512,128]{1,2,0:T(8,128)}) %reduce-scatter.12.cloned.1.call-update) | async-done | bytes 786448 | tf_op jit(solution)/shard_map/reduce_scatter | solution.py:180
  450.6 2.3 copy.51
  452.9 40.1 %all-reduce.5.cloned.1.call-done = f32[128,2048]{1,0:T(8,128)} async-done(((f32[128,2048]{1,0:T(8,128)}), f32[128,2048]{1,0:T(8,128)}) %all-reduce.5.cloned.1.call-update) | async-done | bytes 1048592 | tf_op jit(solution)/shard_map/psum | solution.py:178
  493.0 1.6 fusion.50
  494.6 3.1 fusion.54
  497.7 25.3 %reduce-scatter.14.cloned.1.call-done = f32[128,512]{1,0:T(8,128)} async-done(((f32[128,2048]{1,0:T(8,128)}), f32[128,512]{1,0:T(8,128)}) %reduce-scatter.14.cloned.1.call-update) | async-done | bytes 262160 | tf_op jit(solution)/shard_map/reduce_scatter | solution.py:181
  (126 shorter events, 13.2 us)
Async XLA Ops:
  7.2 191.4 %copy-start = (bf16[1,704,2048]{2,1,0:T(8,128)(2,1)S(1)}, bf16[1,704,2048]{2,1,0:T(8,128)(2,1)}, u32[]{:S(2)}) copy-start(bf16[1,704,2048]{2,1,0:T(8,128)(2,1)} %param.17) | copy-start | bytes 8650756
  7.2 28.9 %all-gather.4.cloned.1.call-start = ((), (), s32[]{:S(2)}) async-start(), calls=%async_computation.8 | async-start | bytes 2621440 | tf_op jit(solution)/shard_map/all_gather | solution.py:73
  10.7 90.3 %reduce-scatter.6.cloned.1.call-start = ((), (), s32[]{:S(2)}) async-start(), calls=%async_computation.9 | async-start | bytes 5242880 | tf_op jit(solution)/shard_map/reduce_scatter | solution.py:91
  39.4 1.7 copy-start.22
  39.7 1.1 copy-start.9
  40.8 1.0 copy-start.13
  44.6 0.7 copy-start.26
  44.6 2.2 copy-start.27
  44.6 2.3 copy-start.7
  52.4 91.0 %copy-start.2 = (bf16[128,2048]{1,0:T(8,128)(2,1)S(1)}, bf16[128,2048]{1,0:T(8,128)(2,1)}, u32[]{:S(2)}) copy-start(bf16[128,2048]{1,0:T(8,128)(2,1)} %param.10) | copy-start | bytes 1572868
  52.4 98.1 %all-to-all-start = ((bf16[16,20,2048]{2,1,0:T(8,128)(2,1)}), bf16[16,20,2048]{2,1,0:T(8,128)(2,1)}, u32[]{:S(2)}, u32[]{:S(2)}) async-start(bf16[16,20,2048]{2,1,0:T(8,128)(2,1)} %reshape.282), calls=%async_computation.1 | async-start | bytes 3145728 | tf_op jit(solution)/shard_map/all_to_all | solution.py:132
  57.2 88.5 %copy-start.25 = (f32[2048]{0:T(1024)S(1)}, f32[2048]{0:T(1024)}, u32[]{:S(2)}) copy-start(f32[2048]{0:T(1024)} %param.15) | copy-start | bytes 24580
  57.2 86.2 %all-reduce.3.cloned.1.call-start = ((), (), s32[]{:S(2)}) async-start(), calls=%async_computation.10 | async-start | bytes 2097152 | tf_op jit(solution)/shard_map/psum | solution.py:97
  144.9 0.8 copy-start.3
  150.5 37.7 %all-to-all-start.1 = ((bf16[16,20,2048]{2,1,0:T(8,128)(2,1)}), bf16[16,20,2048]{2,1,0:T(8,128)(2,1)}, u32[]{:S(2)}, u32[]{:S(2)}) async-start(bf16[16,20,2048]{2,1,0:T(8,128)(2,1)} %reshape.285), calls=%async_computation.2 | async-start | bytes 3145728 | tf_op jit(solution)/shard_map/all_to_all | solution.py:131
  156.2 89.4 %reduce-scatter.8.cloned.1.call-start = ((), (), s32[]{:S(2)}) async-start(), calls=%async_computation.11 | async-start | bytes 3932160 | tf_op jit(solution)/shard_map/reduce_scatter | solution.py:135
  191.5 3.5 copy-start.18
  195.1 3.5 copy-start.31
  195.1 3.5 copy-start.16
  195.1 5.1 slice-start
  198.6 1.6 copy-start.33
  198.6 1.8 slice-start.1
  200.2 1.4 copy-start.28
  200.2 1.4 copy-start.30
  204.4 103.2 %all-gather.6.cloned.1.call-start = ((), (), s32[]{:S(2)}) async-start(), calls=%async_computation.12 | async-start | bytes 2359296 | tf_op jit(solution)/shard_map/all_gather | solution.py:139
  282.6 27.3 %copy-start.4 = (bf16[128,2048]{1,0:T(8,128)(2,1)S(1)}, bf16[128,2048]{1,0:T(8,128)(2,1)}, u32[]{:S(2)}) copy-start(bf16[128,2048]{1,0:T(8,128)(2,1)} %copy-done.3) | copy-start | bytes 1572868
  282.6 52.3 %all-gather.8.cloned.1.call-start = ((), (), s32[]{:S(2)}) async-start(), calls=%async_computation.13 | async-start | bytes 2621440 | tf_op jit(solution)/shard_map/all_gather | solution.py:148
  309.9 1.0 copy-start.8
  310.5 26.7 %copy-start.5 = (f32[128,2048]{1,0:T(8,128)}, f32[128,2048]{1,0:T(8,128)S(1)}, u32[]{:S(2)}) copy-start(f32[128,2048]{1,0:T(8,128)S(1)} %get-tuple-element.37) | copy-start | bytes 3145732
  310.5 24.4 %copy-start.14 = (bf16[128,2048]{1,0:T(8,128)(2,1)S(1)}, bf16[128,2048]{1,0:T(8,128)(2,1)}, u32[]{:S(2)}) copy-start(bf16[128,2048]{1,0:T(8,128)(2,1)} %param.13) | copy-start | bytes 1572868
  312.1 25.1 %copy-start.10 = (f32[512,512]{0,1:T(8,128)S(1)}, f32[512,512]{0,1:T(8,128)}, u32[]{:S(2)}) copy-start(f32[512,512]{0,1:T(8,128)} %copy-done.9) | copy-start | bytes 3145732
  312.2 75.8 %reduce-scatter.10.cloned.1.call-start = ((), (), s32[]{:S(2)}) async-start(), calls=%async_computation.14 | async-start | bytes 5242880 | tf_op jit(solution)/shard_map/reduce_scatter | solution.py:172
  337.2 1.0 copy-start.23
  338.6 1.4 copy-start.15
  343.3 1.6 copy-start.12
  343.3 107.3 %reduce-scatter.12.cloned.1.call-start = ((), (), s32[]{:S(2)}) async-start(), calls=%async_computation.16 | async-start | bytes 3932160 | tf_op jit(solution)/shard_map/reduce_scatter | solution.py:180
  347.5 40.8 %copy-start.6 = (bf16[512,2048]{1,0:T(8,128)(2,1)S(1)}, bf16[512,2048]{1,0:T(8,128)(2,1)}, u32[]{:S(2)}) copy-start(bf16[512,2048]{1,0:T(8,128)(2,1)} %all-gather.8.cloned.1.call-done) | copy-start | bytes 6291460
  347.5 40.8 %copy-start.21 = (bf16[512,128]{0,1:T(8,128)(2,1)S(1)}, bf16[512,128]{0,1:T(8,128)(2,1)}, u32[]{:S(2)}) copy-start(bf16[512,128]{0,1:T(8,128)(2,1)} %copy-done.20) | copy-start | bytes 393220
  347.5 145.5 %all-reduce.5.cloned.1.call-start = ((), (), s32[]{:S(2)}) async-start(), calls=%async_computation.15 | async-start | bytes 2097152 | tf_op jit(solution)/shard_map/psum | solution.py:178
  388.0 135.0 %reduce-scatter.14.cloned.1.call-start = ((), (), s32[]{:S(2)}) async-start(), calls=%async_computation.17 | async-start | bytes 1310720 | tf_op jit(solution)/shard_map/reduce_scatter | solution.py:181
  389.8 3.3 copy-start.19
  389.8 3.3 copy-start.29
  394.8 3.1 copy-start.17
  394.9 3.1 copy-start.32
  394.9 3.2 copy-start.34
  398.1 94.9 %copy-start.24 = (f32[2048]{0:T(1024)S(1)}, f32[2048]{0:T(1024)}, u32[]{:S(2)}) copy-start(f32[2048]{0:T(1024)} %param.14) | copy-start | bytes 24580
  493.0 1.6 copy-start.11
  494.6 28.4 %copy-start.1 = (bf16[1,704,2048]{2,1,0:T(8,128)(2,1)S(1)}, bf16[1,704,2048]{2,1,0:T(8,128)(2,1)}, u32[]{:S(2)}) copy-start(bf16[1,704,2048]{2,1,0:T(8,128)(2,1)} %param.17) | copy-start | bytes 8650756
  (1 other events, 0.7 us)
Sparse Core Ops, SparseCore 0:
  10.8 25.2 all-gather.3
  44.7 56.2 reduce-scatter.5
  103.4 39.9 all-reduce.2
  204.5 41.0 reduce-scatter.7
  282.7 24.8 all-gather.5
  312.3 22.5 all-gather.7
  343.4 44.5 reduce-scatter.9
  390.3 60.2 reduce-scatter.11
  452.9 40.0 all-reduce.4
  495.8 27.1 reduce-scatter.13
where the time goes:
time: 531 us; the launch traced here: 530 us
  waiting for transfers between devices  384 us (72%)
  matrix products  42.7 us (8%)
  local copies, waits for them, and re-layouts  32.4 us (6%)
  blocking collectives  23.6 us (4%)
  other arithmetic  21 us (4%)
  between operations  14.7 us (3%)
  starting transfers between devices  11.3 us (2%)
    reduce_scatter x1, waiting for transfers between devices, body(): lax.psum_scatter(grad_proj, 'dp', scatter_dimension=1, tiled=True)  49.1 us
    reduce_scatter x1, waiting for transfers between devices, body(): lax.psum_scatter(jnp.dot(mixed, w_attn_out, preferred_element_type=jnp.fl...  43.8 us
    psum x1, waiting for transfers between devices, body(): attn_sum = lax.psum(attn_part, 'group')  42.4 us
    reduce_scatter x1, waiting for transfers between devices, body(): lax.psum_scatter(returned, 'group', scatter_dimension=2, tiled=True)  41.2 us
    reduce_scatter x1, waiting for transfers between devices, body(): lax.psum_scatter(jnp.einsum('irh,idh->rd', grad_acts, w_qkv, preferred_el...  40.4 us
    psum x1, waiting for transfers between devices, body(): grad_normed_one = lax.psum(input_part, 'group')  40.1 us
    all_to_all x1, waiting for transfers between devices, body(): lax.all_to_all(send_rows, ('dp', 'head'), split_axis=0, concat_axis=1, ti...  28.5 us
    all_gather x1, waiting for transfers between devices, body(): shard_rows = lax.all_gather(normed_one, 'head', axis=0, tiled=True)  25.4 us
  transfers between devices with their start and end apart: 12, of which 11 were waited for; matrix products, arithmetic and copies ran while one was open for 7% of the time, Pallas kernels for 0%

commit v1 on v0

--- a/solution.py
+++ b/solution.py
@@ -1,10 +1,15 @@
 import jax
 import jax.numpy as jnp
 from jax import lax
+from jax.experimental import pallas as pl
+from jax.experimental.pallas import tpu as pltpu
 from jax.sharding import PartitionSpec as P
 
 HD = 128
 
+
+MESH = pl.DeviceIdType.MESH
+VMEM_LIMIT = 48 * 1024 * 1024
 
 epsilon = 1e-06
 
@@ -60,6 +65,231 @@
     return (grad_pair, grad_down, returned)
 
 
+def span(block, size, part=0, length=None):
+    length = size if length is None else length
+    return pl.ds(pl.multiple_of(block * size + part * length, length), length)
+
+
+def greet(peers):
+    barrier = pltpu.get_barrier_semaphore()
+    for peer in peers:
+        pl.semaphore_signal(barrier, inc=1, device_id=peer, device_id_type=MESH)
+    pl.semaphore_wait(barrier, len(peers))
+
+
+def remote(src, dst, send_sem, recv_sem, peer):
+    return pltpu.make_async_remote_copy(
+        src_ref=src, dst_ref=dst, send_sem=send_sem, recv_sem=recv_sem,
+        device_id=peer, device_id_type=MESH,
+    )
+
+
+def comm_call(kernel, out, scratch, collective_id, *operands):
+    return pl.pallas_call(
+        kernel,
+        out_shape=out,
+        in_specs=[pl.BlockSpec(memory_space=pltpu.VMEM)] * len(operands),
+        out_specs=pl.BlockSpec(memory_space=pltpu.VMEM),
+        scratch_shapes=scratch,
+        compiler_params=pltpu.CompilerParams(
+            collective_id=collective_id, has_side_effects=True, vmem_limit_bytes=VMEM_LIMIT
+        ),
+    )(*operands)
+
+
+def head_peers(count):
+    me = lax.axis_index("head")
+    mate = me + 1 - 2 * lax.rem(me, 2)
+    return me, mate, [lax.rem(me + 2 * j, count) for j in range(1, count // 2)]
+
+
+def gather_head(block, collective_id):
+    rows, width = block.shape
+    count = lax.axis_size("head")
+    chunks = 4
+    part = rows // chunks
+    others = count // 2 - 1
+
+    def kernel(x_ref, o_ref, far_send, far_recv, own_send, own_recv, on_send, on_recv):
+        me, mate, far = head_peers(count)
+        greet([{"head": mate}] + [{"head": f} for f in far])
+        sends, passed = [], []
+        for c in range(chunks):
+            for j, f in enumerate(far):
+                copy = remote(x_ref.at[pl.ds(c * part, part)], o_ref.at[span(me, rows, c, part)],
+                              far_send.at[j, c], far_recv.at[j, c], {"head": f})
+                copy.start()
+                sends.append(copy)
+        own = remote(x_ref, o_ref.at[span(me, rows)], own_send, own_recv, {"head": mate})
+        own.start()
+        o_ref[span(me, rows)] = x_ref[...]
+        for c in range(chunks):
+            for j in range(others):
+                source = lax.rem(me + count - 2 * (j + 1), count)
+                place = o_ref.at[span(source, rows, c, part)]
+                remote(place, place, far_send.at[j, c], far_recv.at[j, c], {"head": mate}).wait_recv()
+                copy = remote(place, place, on_send.at[j, c], on_recv.at[j, c], {"head": mate})
+                copy.start()
+                passed.append(copy)
+        place = o_ref.at[span(mate, rows)]
+        remote(place, place, own_send, own_recv, {"head": mate}).wait_recv()
+        for c in range(chunks):
+            for j in range(others):
+                source = lax.rem(mate + count - 2 * (j + 1), count)
+                place = o_ref.at[span(source, rows, c, part)]
+                remote(place, place, on_send.at[j, c], on_recv.at[j, c], {"head": mate}).wait_recv()
+        own.wait_send()
+        for copy in sends + passed:
+            copy.wait_send()
+
+    dma = pltpu.SemaphoreType.DMA
+    many = dma((max(others, 1), chunks))
+    return comm_call(
+        kernel, jax.ShapeDtypeStruct((count * rows, width), block.dtype),
+        [many, many, dma, dma, many, many], collective_id, block,
+    )
+
+
+def sum_to_rows(partial, collective_id):
+    count, groups = lax.axis_size("head"), lax.axis_size("group")
+    rows, width = partial.shape[0] // count, partial.shape[1]
+    chunks = 4
+    part = rows // chunks
+    pairs = count // 2
+
+    def kernel(p_ref, o_ref, mate_in, far_out, far_in, all_in,
+               mate_send, mate_recv, far_send, far_recv, group_send, group_recv):
+        me, mate, far = head_peers(count)
+        group = lax.axis_index("group")
+        rest = [lax.rem(group + k, groups) for k in range(1, groups)]
+        greet([{"head": mate}] + [{"head": f} for f in far] + [{"group": g} for g in rest])
+        order = list(range(1, pairs)) + [0]
+        copies = []
+        mates = {}
+        for c in range(chunks):
+            for j in order:
+                block = lax.rem(mate + 2 * j, count)
+                copy = remote(p_ref.at[span(block, rows, c, part)],
+                              mate_in.at[j, pl.ds(c * part, part)],
+                              mate_send.at[j, c], mate_recv.at[j, c], {"head": mate})
+                copy.start()
+                mates[j, c] = copy
+                copies.append(copy)
+        fars = {}
+        for c in range(chunks):
+            at = pl.ds(c * part, part)
+            for j in range(1, pairs):
+                mates[j, c].wait_recv()
+                mine = p_ref[span(far[j - 1], rows, c, part)].astype(jnp.float32)
+                far_out[j - 1, at] = (mine + mate_in[j, at].astype(jnp.float32)).astype(jnp.bfloat16)
+                copy = remote(far_out.at[j - 1, at], far_in.at[j - 1, at],
+                              far_send.at[j - 1, c], far_recv.at[j - 1, c], {"head": far[j - 1]})
+                copy.start()
+                fars[j, c] = copy
+                copies.append(copy)
+        crossing = {}
+        for c in range(chunks):
+            at = pl.ds(c * part, part)
+            mates[0, c].wait_recv()
+            total = p_ref[span(me, rows, c, part)].astype(jnp.float32)
+            total = total + mate_in[0, at].astype(jnp.float32)
+            for j in range(1, pairs):
+                fars[j, c].wait_recv()
+                total = total + far_in[j - 1, at].astype(jnp.float32)
+            all_in[group, at] = total.astype(jnp.bfloat16)
+            for k, g in enumerate(rest):
+                copy = remote(all_in.at[group, at], all_in.at[group, at],
+                              group_send.at[k, c], group_recv.at[k, c], {"group": g})
+                copy.start()
+                crossing[k, c] = copy
+                copies.append(copy)
+        for c in range(chunks):
+            at = pl.ds(c * part, part)
+            for k in range(groups - 1):
+                source = lax.rem(group + groups - k - 1, groups)
+                place = all_in.at[source, at]
+                remote(place, place, group_send.at[k, c], group_recv.at[k, c],
+                       {"group": rest[k]}).wait_recv()
+            total = all_in[0, at].astype(jnp.float32)
+            for g in range(1, groups):
+                total = total + all_in[g, at].astype(jnp.float32)
+            o_ref[at] = total
+        for copy in copies:
+            copy.wait_send()
+
+    dma = pltpu.SemaphoreType.DMA
+    b16 = jnp.bfloat16
+    mate_sem, far_sem = dma((pairs, chunks)), dma((max(pairs - 1, 1), chunks))
+    group_sem = dma((max(groups - 1, 1), chunks))
+    return comm_call(
+        kernel, jax.ShapeDtypeStruct((rows, width), jnp.float32),
+        [pltpu.VMEM((pairs, rows, width), b16), pltpu.VMEM((max(pairs - 1, 1), rows, width), b16),
+         pltpu.VMEM((max(pairs - 1, 1), rows, width), b16), pltpu.VMEM((groups, rows, width), b16),
+         mate_sem, mate_sem, far_sem, far_sem, group_sem, group_sem],
+        collective_id, partial,
+    )
+
+
+def sum_to_columns(partial, collective_id):
+    groups = lax.axis_size("group")
+    rows, width = partial.shape
+    share = width // groups
+
+    def kernel(p_ref, o_ref, landed, send, recv):
+        group = lax.axis_index("group")
+        rest = [lax.rem(group + k, groups) for k in range(1, groups)]
+        greet([{"group": g} for g in rest])
+        copies = []
+        for k, g in enumerate(rest):
+            copy = remote(p_ref.at[:, span(g, share)], landed.at[k], send.at[k], recv.at[k],
+                          {"group": g})
+            copy.start()
+            copies.append(copy)
+        total = p_ref[:, span(group, share)].astype(jnp.float32)
+        for k, copy in enumerate(copies):
+            copy.wait_recv()
+            total = total + landed[k].astype(jnp.float32)
+        o_ref[...] = total.astype(jnp.bfloat16)
+        for copy in copies:
+            copy.wait_send()
+
+    dma = pltpu.SemaphoreType.DMA((max(groups - 1, 1),))
+    return comm_call(
+        kernel, jax.ShapeDtypeStruct((rows, share), jnp.bfloat16),
+        [pltpu.VMEM((max(groups - 1, 1), rows, share), jnp.bfloat16), dma, dma],
+        collective_id, partial,
+    )
+
+
+def gather_columns(block, collective_id):
+    groups = lax.axis_size("group")
+    rows, share = block.shape
+
+    def kernel(x_ref, o_ref, send, recv):
+        group = lax.axis_index("group")
+        rest = [lax.rem(group + k, groups) for k in range(1, groups)]
+        greet([{"group": g} for g in rest])
+        copies = []
+        for k, g in enumerate(rest):
+            copy = remote(x_ref, o_ref.at[:, span(group, share)], send.at[k], recv.at[k],
+                          {"group": g})
+            copy.start()
+            copies.append(copy)
+        o_ref[:, span(group, share)] = x_ref[...]
+        for k in range(groups - 1):
+            source = lax.rem(group + groups - k - 1, groups)
+            place = o_ref.at[:, span(source, share)]
+            remote(place, place, send.at[k], recv.at[k], {"group": rest[k]}).wait_recv()
+        for copy in copies:
+            copy.wait_send()
+
+    dma = pltpu.SemaphoreType.DMA((max(groups - 1, 1),))
+    return comm_call(
+        kernel, jax.ShapeDtypeStruct((rows, groups * share), block.dtype), [dma, dma],
+        collective_id, block,
+    )
+
+
 def body(
     tokens, grad_out, w_qkv, w_attn_out, gain_attn, gain_ffn, w_gate_up, w_down, expert_ids, gates
 ):
@@ -70,7 +300,7 @@
     tokens_f = tokens.astype(jnp.float32)
     scale_one = inverse_rms(tokens_f)
     normed_one = (tokens_f * scale_one * gain_attn).astype(jnp.bfloat16)
-    shard_rows = lax.all_gather(normed_one, "head", axis=0, tiled=True)
+    shard_rows = gather_head(normed_one, 0)
     fresh = jnp.einsum("rd,idh->irh", shard_rows, w_qkv, preferred_element_type=jnp.float32).astype(
         jnp.bfloat16
     )
@@ -88,13 +318,9 @@
         .astype(jnp.bfloat16)
         .reshape(seq_len, head_cols)
     )
-    attn_part = lax.psum_scatter(
-        jnp.dot(mixed, w_attn_out, preferred_element_type=jnp.float32),
-        "head",
-        scatter_dimension=0,
-        tiled=True,
-    )
-    attn_sum = lax.psum(attn_part, "group")
+    attn_sum = sum_to_rows(
+        jnp.dot(mixed, w_attn_out, preferred_element_type=jnp.float32).astype(jnp.bfloat16), 1
+    )
     hidden = (tokens_f + attn_sum).astype(jnp.bfloat16)
     hidden_f = hidden.astype(jnp.float32)
     scale_two = inverse_rms(hidden_f)
@@ -132,20 +358,24 @@
         lax.all_to_all(send_grads, ("dp", "head"), split_axis=0, concat_axis=1, tiled=True),
     )
     grad_pair, grad_down, returned = expert_work(got_rows, got_grads, w_gate_up, w_down)
-    shared = lax.psum_scatter(returned, "group", scatter_dimension=2, tiled=True)
+    shared = sum_to_columns(
+        returned.astype(jnp.bfloat16).reshape(expert_count * capacity, width), 2
+    ).reshape(local_count, owners * capacity, -1)
     back_half = lax.all_to_all(
-        shared.astype(jnp.bfloat16), ("dp", "head"), split_axis=1, concat_axis=0, tiled=True
-    )
-    back_rows = lax.all_gather(back_half, "group", axis=2, tiled=True)
-    grad_normed = jnp.einsum(
-        "cr,cd->rd",
-        picker,
-        back_rows.reshape(expert_count * capacity, width),
-        preferred_element_type=jnp.float32,
-    )
+        shared, ("dp", "head"), split_axis=1, concat_axis=0, tiled=True
+    )
+    grad_normed = gather_columns(
+        jnp.einsum(
+            "cr,cd->rd",
+            picker,
+            back_half.reshape(expert_count * capacity, -1),
+            preferred_element_type=jnp.float32,
+        ).astype(jnp.bfloat16),
+        3,
+    ).astype(jnp.float32)
     grad_hidden = grad_f + norm_backward(hidden_f, scale_two, gain_ffn, grad_normed)
     grad_hidden_b = grad_hidden.astype(jnp.bfloat16)
-    shard_rows = lax.all_gather(grad_hidden_b, "head", axis=0, tiled=True)
+    shard_rows = gather_head(grad_hidden_b, 4)
     weight_total = jnp.einsum("rh,rd->hd", mixed, shard_rows, preferred_element_type=jnp.float32)
     fresh = jnp.einsum(
         "rd,hd->rh", shard_rows, w_attn_out, preferred_element_type=jnp.float32
@@ -169,16 +399,19 @@
     ).astype(jnp.bfloat16)
     grad_acts = jnp.stack([grad_queries, grad_keys, grad_values]).reshape(3, seq_len, head_cols)
     grad_proj = jnp.einsum("sd,ish->idh", normed_all, grad_acts, preferred_element_type=jnp.float32)
-    input_part = lax.psum_scatter(
-        jnp.einsum("irh,idh->rd", grad_acts, w_qkv, preferred_element_type=jnp.float32),
-        "head",
-        scatter_dimension=0,
-        tiled=True,
-    )
-    grad_normed_one = lax.psum(input_part, "group")
+    grad_normed_one = sum_to_rows(
+        jnp.einsum("irh,idh->rd", grad_acts, w_qkv, preferred_element_type=jnp.float32).astype(
+            jnp.bfloat16
+        ),
+        5,
+    )
     grad_proj_sum, grad_out_sum = (
-        lax.psum_scatter(grad_proj, "dp", scatter_dimension=1, tiled=True),
-        lax.psum_scatter(grad_out_w, "dp", scatter_dimension=1, tiled=True),
+        lax.psum_scatter(
+            grad_proj.astype(jnp.bfloat16), "dp", scatter_dimension=1, tiled=True
+        ).astype(jnp.float32),
+        lax.psum_scatter(
+            grad_out_w.astype(jnp.bfloat16), "dp", scatter_dimension=1, tiled=True
+        ).astype(jnp.float32),
     )
     grad_tokens = (
         grad_hidden + norm_backward(tokens_f, scale_one, gain_attn, grad_normed_one)

time: 531 us -> 300 us (0.56)
  waiting for transfers between devices: 384 us -> 57.8 us
  Pallas kernels: 0 us -> 99 us
  local copies, waits for them, and re-layouts: 32.4 us -> 25.5 us
    reduce_scatter x5 -> x2, waiting for transfers between devices: 200 us -> 11.9 us  [the longest x1 11.9 us: body(): lax.psum_scatter(grad_proj.astype(jnp.bfloat16), 'dp', scatter_dimension=...]
    pallas_call x0 -> x6, Pallas kernels: none -> 99 us  [comm_call(): pl.pallas_call(kernel, out_shape=out, in_specs=[pl.BlockSpec(memory_space...]
    psum x2 -> x0, waiting for transfers between devices: 82.5 us -> none  [the longest x1 42.4 us: body(): attn_sum = lax.psum(attn_part, 'group')]
    all_gather x3 -> x0, waiting for transfers between devices: 73 us -> none  [the longest x1 25.4 us: body(): shard_rows = lax.all_gather(normed_one, 'head', axis=0, tiled=True)]
    all_to_all x1, waiting for transfers between devices: 0.01 us -> 20 us  [body(): lax.all_to_all(send_grads, ('dp', 'head'), split_axis=0, concat_axis=1, t...]
    unnamed x79 -> x97, local copies, waits for them, and re-layouts: 10.5 us -> 10.9 us
  transfers between devices with their start and end apart: 12 -> 4, of which waited for: 11 -> 3; matrix products, arithmetic and copies ran while one was open for 7% -> 13% of each run, Pallas kernels for 0% -> 7%
where the time goes in v1:
time: 300 us; the launch traced here: 299 us
  Pallas kernels  99 us (33%)
  waiting for transfers between devices  57.8 us (19%)
  matrix products  42.8 us (14%)
  blocking collectives  26.7 us (9%)
  local copies, waits for them, and re-layouts  25.5 us (8%)
  other arithmetic  17.2 us (6%)
  starting transfers between devices  15.1 us (5%)
  between operations  14.7 us (5%)
    pallas_call x6, Pallas kernels, comm_call(): pl.pallas_call(kernel, out_shape=out, in_specs=[pl.BlockSpec(memory_space...  99 us
    all_to_all x1, blocking collectives, body(): lax.all_to_all(shared, ('dp', 'head'), split_axis=1, concat_axis=0, tiled...  26.7 us
    all_to_all x1, waiting for transfers between devices, body(): lax.all_to_all(send_rows, ('dp', 'head'), split_axis=0, concat_axis=1, ti...  25.8 us
    all_to_all x1, waiting for transfers between devices, body(): lax.all_to_all(send_grads, ('dp', 'head'), split_axis=0, concat_axis=1, t...  20 us
    reduce_scatter x1, waiting for transfers between devices, body(): lax.psum_scatter(grad_proj.astype(jnp.bfloat16), 'dp', scatter_dimension=...  11.9 us
    unnamed x97, local copies, waits for them, and re-layouts  10.9 us
    all_to_all x1, starting transfers between devices, body(): lax.all_to_all(send_grads, ('dp', 'head'), split_axis=0, concat_axis=1, t...  9.15 us
    another operation x3, local copies, waits for them, and re-layouts  6.58 us
  transfers between devices with their start and end apart: 4, of which 3 were waited for; matrix products, arithmetic and copies ran while one was open for 13% of the time, Pallas kernels for 7%

profile of v1, /device:TPU:0, one launch (start us, length us, event | category | flops | bytes accessed | tf_op | source)
XLA Modules:
  0.0 298.8 jit_solution(4935059735786872646)
XLA Ops:
  7.2 0.9 copy.54
  8.4 1.2 fusion.56
  10.8 0.8 multiply_add_fusion
  11.7 1.2 fusion.50.x_ref
  12.9 16.7 %shard_map.137 = bf16[512,2048]{1,0:T(8,128)(2,1)S(1)} custom-call(bf16[128,2048]{1,0:T(8,128)(2,1)S(1)} %fusion.50.x_ref), custom_call_target="tpu_custom_call" | custom-call | tf_op jit(solution)/shard_map/pallas_call | solution.py:88
  29.7 1.3 fusion.37
  33.3 0.7 convolution_convert_fusion.3.p_ref
  34.1 20.9 %shard_map.138 = f32[128,2048]{1,0:T(8,128)S(1)} custom-call(bf16[512,2048]{1,0:T(8,128)(2,1)S(1)} %convolution_convert_fusion.3.p_ref), custom_call_target="tpu_custom_call" | custom-call | tf_op jit(solution)/shard_map/pallas_call | solution.py:88
  55.3 0.8 copy-done.6
  56.1 1.7 convolution_convert_fusion.5
  57.8 3.2 %reshape.292 = bf16[16,20,2048]{2,1,0:T(8,128)(2,1)} reshape(bf16[320,2048]{1,0:T(8,128)(2,1)} %convolution_convert_fusion.5) | data formatting | bytes 2621440 | tf_op jit(solution)/shard_map/reshape | solution.py:347
  61.0 5.7 %all-to-all-start.1 = ((bf16[16,20,2048]{2,1,0:T(8,128)(2,1)}), bf16[16,20,2048]{2,1,0:T(8,128)(2,1)}, u32[]{:S(2)}, u32[]{:S(2)}) async-start(bf16[16,20,2048]{2,1,0:T(8,128)(2,1)} %reshape.292), calls=%async_computation.1 | async-start | bytes 3145728 | tf_op jit(solution)/shard_map/all_to_all | solution.py:357
  66.6 0.7 select_reduce_fusion
  67.4 2.3 convolution_convert_fusion.6
  69.6 3.2 %reshape.289 = bf16[16,20,2048]{2,1,0:T(8,128)(2,1)} reshape(bf16[320,2048]{1,0:T(8,128)(2,1)} %convolution_convert_fusion.6) | data formatting | bytes 2621440 | tf_op jit(solution)/shard_map/reshape | solution.py:354
  72.9 25.8 %all-to-all-done.1 = bf16[16,20,2048]{2,1,0:T(8,128)(2,1)} async-done(((bf16[16,20,2048]{2,1,0:T(8,128)(2,1)}), bf16[16,20,2048]{2,1,0:T(8,128)(2,1)}, u32[]{:S(2)}, u32[]{:S(2)}) %all-to-all-start.1) | async-done | bytes 1310752 | tf_op jit(solution)/shard_map/all_to_all | solution.py:357
  98.7 9.2 %all-to-all-start = ((bf16[16,20,2048]{2,1,0:T(8,128)(2,1)}), bf16[16,20,2048]{2,1,0:T(8,128)(2,1)}, u32[]{:S(2)}, u32[]{:S(2)}) async-start(bf16[16,20,2048]{2,1,0:T(8,128)(2,1)} %reshape.289), calls=%async_computation | async-start | bytes 3145728 | tf_op jit(solution)/shard_map/all_to_all | solution.py:358
  108.1 3.3 %reshape.293 = bf16[320,2048]{1,0:T(8,128)(2,1)} reshape(bf16[16,20,2048]{2,1,0:T(8,128)(2,1)} %all-to-all-done.1) | data formatting | bytes 2621440 | tf_op jit(solution)/shard_map/reshape.40
  111.3 4.5 %fusion.5 = f32[320,704]{1,0:T(8,128)} fusion(bf16[320,2048]{1,0:T(8,128)(2,1)} %reshape.293, bf16[1,2,2048,704]{2,3,1,0:T(8,128)(2,1)} %param.16), kind=kOutput, calls=%fused_computation.11 | convolution fusion | flops 922746880 | bytes 5095424 | tf_op jit(solution)/shard_map/esd,edf->esf/dot_general | solution.py:43
  115.9 4.0 %fusion.9 = f32[320,704]{1,0:T(8,128)} fusion(bf16[320,2048]{1,0:T(8,128)(2,1)S(1)} %copy-done.17, bf16[1,2,2048,704]{2,3,1,0:T(8,128)(2,1)} %param.16), kind=kOutput, calls=%fused_computation.15 | convolution fusion | flops 922746880 | bytes 5095424 | tf_op jit(solution)/shard_map/esd,edf->esf/dot_general | solution.py:44
  119.9 20.0 %all-to-all-done = bf16[16,20,2048]{2,1,0:T(8,128)(2,1)} async-done(((bf16[16,20,2048]{2,1,0:T(8,128)(2,1)}), bf16[16,20,2048]{2,1,0:T(8,128)(2,1)}, u32[]{:S(2)}, u32[]{:S(2)}) %all-to-all-start) | async-done | bytes 1310752 | tf_op jit(solution)/shard_map/all_to_all | solution.py:358
  139.9 3.3 %reshape.290 = bf16[320,2048]{1,0:T(8,128)(2,1)} reshape(bf16[16,20,2048]{2,1,0:T(8,128)(2,1)} %all-to-all-done) | data formatting | bytes 2621440 | tf_op jit(solution)/shard_map/reshape.35
  143.2 3.3 %multiply_convert_fusion.2 = (bf16[320,704]{1,0:T(8,128)(2,1)S(1)}, bf16[320,704]{1,0:T(8,128)(2,1)S(1)}) fusion(f32[320,704]{1,0:T(8,128)} %fusion.5, f32[320,704]{1,0:T(8,128)} %fusion.9, bf16[320,2048]{1,0:T(8,128)(2,1)} %reshape.290, bf16[1,704,2048]{2,1,0:T(8,128)(2,1)S(1)} %copy-done), kind=kOutput, calls=%fused_computation.78 | convolution fusion | flops 925675520 | bytes 6897664 | tf_op jit(solution)/shard_map/esd,efd->esf/dot_general | solution.py:48
  146.5 3.4 %fusion.3 = f32[320,2048]{1,0:T(8,128)S(1)} fusion(bf16[320,704]{1,0:T(8,128)(2,1)S(1)} %get-tuple-element.38, bf16[1,2,2048,704]{2,3,1,0:T(8,128)(2,1)} %param.16), kind=kOutput, calls=%fused_computation.9 | convolution fusion | flops 922746880 | bytes 5955584 | tf_op jit(solution)/shard_map/esf,edf->esd/dot_general | solution.py:61
  149.9 3.1 %fusion.16.p_ref = bf16[320,2048]{1,0:T(8,128)(2,1)S(1)} fusion(f32[320,2048]{1,0:T(8,128)S(1)} %fusion.3, bf16[320,704]{1,0:T(8,128)(2,1)S(1)} %get-tuple-element.37, bf16[1,2,2048,704]{2,3,1,0:T(8,128)(2,1)} %param.16), kind=kOutput, calls=%fused_computation.23 | convolution fusion | flops 924057600 | bytes 7266304 | tf_op jit(solution)/shard_map/esf,edf->esd/dot_general | solution.py:62
  153.0 17.6 %shard_map.139 = bf16[320,1024]{1,0:T(8,128)(2,1)S(1)} custom-call(bf16[320,2048]{1,0:T(8,128)(2,1)S(1)} %fusion.16.p_ref), custom_call_target="tpu_custom_call" | custom-call | tf_op jit(solution)/shard_map/pallas_call | solution.py:88
  170.6 1.0 copy.70
  172.1 4.5 %reduce.8 = bf16[320,1024]{1,0:T(8,128)(2,1)S(1)} reduce(bf16[320,1,1024]{2,1,0:T(2,128)(2,1)S(1)} %bitcast.140, bf16[]{:T(256)} %broadcast.113), dimensions={1}, to_apply=%bitcast.138.reduce_sub_computation | reduce | bytes 1310722
  177.0 26.7 %all_to_all.12 = bf16[16,2,10240]{2,1,0:T(2,128)(2,1)S(1)} all-to-all(bf16[16,2,10240]{2,1,0:T(2,128)(2,1)S(1)} %reshape.302), channel_id=1, replica_groups=mesh['dp'=4,'head'=4,'group'=2] {'dp','head'}, dimensions={0} | all-to-all | bytes 1310720 | tf_op jit(solution)/shard_map/all_to_all | solution.py:364
  203.7 1.9 reshape.303
  205.7 1.7 convolution_convert_fusion.8.x_ref
  207.4 8.6 %shard_map.140 = bf16[128,2048]{1,0:T(8,128)(2,1)S(1)} custom-call(bf16[128,1024]{1,0:T(8,128)(2,1)S(1)} %convolution_convert_fusion.8.x_ref), custom_call_target="tpu_custom_call" | custom-call | tf_op jit(solution)/shard_map/pallas_call | solution.py:88
  217.2 14.5 %shard_map.141 = bf16[512,2048]{1,0:T(8,128)(2,1)S(1)} custom-call(bf16[128,2048]{1,0:T(8,128)(2,1)S(1)} %fusion.71.x_ref), custom_call_target="tpu_custom_call" | custom-call | tf_op jit(solution)/shard_map/pallas_call | solution.py:88
  231.8 0.7 convolution_convert_fusion.12
  232.5 1.2 convolution_convert_fusion.7
  233.8 1.7 multiply_reduce_fusion
  237.8 1.1 copy-done.3
  238.9 2.2 fusion.19
  241.1 3.3 %fusion.1 = bf16[1,1,2048,704]{2,3,1,0:T(8,128)(2,1)S(1)} fusion(bf16[320,2048]{1,0:T(8,128)(2,1)} %reshape.293, bf16[320,704]{1,0:T(8,128)(2,1)} %copy-done.43), kind=kOutput, calls=%fused_computation.7 | convolution fusion | flops 924188672 | bytes 4644864 | tf_op jit(solution)/shard_map/esd,esf->edf/dot_general | solution.py:57
  244.3 1.7 fusion
  246.1 3.0 %pad_maximum_fusion = bf16[1,2,2048,704]{2,3,1,0:T(8,128)(2,1)} fusion(bf16[1,1,2048,704]{2,3,1,0:T(8,128)(2,1)S(1)} %fusion.1, bf16[1,1,2048,704]{2,3,1,0:T(8,128)(2,1)S(1)} %fusion), kind=kLoop, calls=%fused_computation | loop fusion | flops 2883584 | bytes 11534336 | tf_op jit(solution)/shard_map/stack | solution.py:54
  249.2 3.3 %fusion.2 = bf16[1,704,2048]{2,1,0:T(8,128)(2,1)} fusion(bf16[320,2048]{1,0:T(8,128)(2,1)S(1)} %copy-done.19, f32[320,704]{1,0:T(8,128)S(1)} %copy-done.45, f32[320,704]{1,0:T(8,128)S(1)} %copy-done.44), kind=kOutput, calls=%fused_computation.8 | convolution fusion | flops 925540352 | bytes 5996544 | tf_op jit(solution)/shard_map/esf,esd->efd/dot_general | solution.py:49
  252.5 1.3 bitcast_convert_fusion.p_ref
  253.9 20.6 %shard_map.142 = f32[128,2048]{1,0:T(8,128)S(1)} custom-call(bf16[512,2048]{1,0:T(8,128)(2,1)S(1)} %bitcast_convert_fusion.p_ref), custom_call_target="tpu_custom_call" | custom-call | tf_op jit(solution)/shard_map/pallas_call | solution.py:88
  274.9 1.4 fusion.55
  276.4 1.6 convert_element_type.189
  278.0 11.9 %reduce-scatter.3.cloned.1.call-done = bf16[3,512,128]{1,2,0:T(8,128)(2,1)} async-done(((bf16[3,2048,128]{1,2,0:T(8,128)(2,1)}), bf16[3,512,128]{1,2,0:T(8,128)(2,1)}) %reduce-scatter.3.cloned.1.call-update) | async-done | bytes 393232 | tf_op jit(solution)/shard_map/reduce_scatter | solution.py:409
  289.9 2.0 copy.60
  (123 shorter events, 9.2 us)
Async XLA Ops:
  7.2 136.0 %copy-start = (bf16[1,704,2048]{2,1,0:T(8,128)(2,1)S(1)}, bf16[1,704,2048]{2,1,0:T(8,128)(2,1)}, u32[]{:S(2)}) copy-start(bf16[1,704,2048]{2,1,0:T(8,128)(2,1)} %param.17) | copy-start | bytes 8650756
  9.6 21.3 %copy-start.33 = (f32[128]{0:T(128)}, f32[128]{0:T(128)S(1)}, u32[]{:S(2)}) copy-start(f32[128]{0:T(128)S(1)} %add_rsqrt_fusion.1) | copy-start | bytes 1540
  10.8 18.9 %copy-start.37 = (bf16[3,2048,128]{2,1,0:T(8,128)(2,1)S(1)}, bf16[3,2048,128]{2,1,0:T(8,128)(2,1)}, u32[]{:S(2)}) copy-start(bf16[3,2048,128]{2,1,0:T(8,128)(2,1)} %param.12) | copy-start | bytes 4718596
  11.7 43.7 %copy-start.22 = (pred[320,128]{1,0:T(8,128)(4,1)}, pred[320,128]{1,0:T(8,128)(4,1)S(1)}, u32[]{:S(2)}) copy-start(pred[320,128]{1,0:T(8,128)(4,1)S(1)} %fusion.66) | copy-start | bytes 122884
  29.7 1.3 copy-start.2
  31.0 0.8 copy-start.20
  31.3 1.0 copy-start.12
  32.3 1.0 copy-start.15
  34.1 21.0 %copy-start.4 = (bf16[128,2048]{1,0:T(8,128)(2,1)S(1)}, bf16[128,2048]{1,0:T(8,128)(2,1)}, u32[]{:S(2)}) copy-start(bf16[128,2048]{1,0:T(8,128)(2,1)} %param.10) | copy-start | bytes 1572868
  34.1 22.0 %copy-start.24 = (f32[2048]{0:T(1024)S(1)}, f32[2048]{0:T(1024)}, u32[]{:S(2)}) copy-start(f32[2048]{0:T(1024)} %param.15) | copy-start | bytes 24580
  55.3 0.8 copy-start.6
  55.3 0.8 copy-start.30
  61.0 6.4 %copy-start.9 = (bf16[128,2048]{1,0:T(8,128)(2,1)S(1)}, bf16[128,2048]{1,0:T(8,128)(2,1)}, u32[]{:S(2)}) copy-start(bf16[128,2048]{1,0:T(8,128)(2,1)} %param.11) | copy-start | bytes 1572868
  61.0 37.7 %all-to-all-start.1 = ((bf16[16,20,2048]{2,1,0:T(8,128)(2,1)}), bf16[16,20,2048]{2,1,0:T(8,128)(2,1)}, u32[]{:S(2)}, u32[]{:S(2)}) async-start(bf16[16,20,2048]{2,1,0:T(8,128)(2,1)} %reshape.292), calls=%async_computation.1 | async-start | bytes 3145728 | tf_op jit(solution)/shard_map/all_to_all | solution.py:357
  98.7 41.2 %all-to-all-start = ((bf16[16,20,2048]{2,1,0:T(8,128)(2,1)}), bf16[16,20,2048]{2,1,0:T(8,128)(2,1)}, u32[]{:S(2)}, u32[]{:S(2)}) async-start(bf16[16,20,2048]{2,1,0:T(8,128)(2,1)} %reshape.289), calls=%async_computation | async-start | bytes 3145728 | tf_op jit(solution)/shard_map/all_to_all | solution.py:358
  107.8 168.5 %reduce-scatter.5.cloned.1.call-start = ((), (), s32[]{:S(2)}) async-start(), calls=%async_computation.6 | async-start | bytes 655360 | tf_op jit(solution)/shard_map/reduce_scatter | solution.py:412
  111.3 4.5 %copy-start.17 = (bf16[320,2048]{1,0:T(8,128)(2,1)S(1)}, bf16[320,2048]{1,0:T(8,128)(2,1)}, u32[]{:S(2)}) copy-start(bf16[320,2048]{1,0:T(8,128)(2,1)} %reshape.293) | copy-start | bytes 3932164
  146.5 3.4 %copy-start.41 = (bf16[320,704]{1,0:T(8,128)(2,1)}, bf16[320,704]{1,0:T(8,128)(2,1)S(1)}, u32[]{:S(2)}) copy-start(bf16[320,704]{1,0:T(8,128)(2,1)S(1)} %get-tuple-element.38) | copy-start | bytes 1351684
  146.5 3.4 %copy-start.43 = (bf16[320,704]{1,0:T(8,128)(2,1)}, bf16[320,704]{1,0:T(8,128)(2,1)S(1)}, u32[]{:S(2)}) copy-start(bf16[320,704]{1,0:T(8,128)(2,1)S(1)} %get-tuple-element.37) | copy-start | bytes 1351684
  176.6 29.1 %copy-start.23 = (pred[320,128]{1,0:T(8,128)(4,1)S(1)}, pred[320,128]{1,0:T(8,128)(4,1)}, u32[]{:S(2)}) copy-start(pred[320,128]{1,0:T(8,128)(4,1)} %copy-done.22) | copy-start | bytes 122884
  203.7 12.3 %copy-start.7 = (bf16[128,2048]{1,0:T(8,128)(2,1)S(1)}, bf16[128,2048]{1,0:T(8,128)(2,1)}, u32[]{:S(2)}) copy-start(bf16[128,2048]{1,0:T(8,128)(2,1)} %copy-done.6) | copy-start | bytes 1572868
  203.7 12.3 %copy-start.31 = (f32[128]{0:T(128)S(1)}, f32[128]{0:T(128)}, u32[]{:S(2)}) copy-start(f32[128]{0:T(128)} %copy-done.30) | copy-start | bytes 1540
  203.7 13.1 %copy-start.10 = (bf16[128,2048]{1,0:T(8,128)(2,1)S(1)}, bf16[128,2048]{1,0:T(8,128)(2,1)}, u32[]{:S(2)}) copy-start(bf16[128,2048]{1,0:T(8,128)(2,1)} %param.11) | copy-start | bytes 1572868
  216.8 15.0 %copy-start.16 = (bf16[128,2048]{1,0:T(8,128)(2,1)S(1)}, bf16[128,2048]{1,0:T(8,128)(2,1)}, u32[]{:S(2)}) copy-start(bf16[128,2048]{1,0:T(8,128)(2,1)} %param.13) | copy-start | bytes 1572868
  232.5 1.3 copy-start.29
  233.8 1.8 copy-start.13
  233.8 56.1 %reduce-scatter.3.cloned.1.call-start = ((), (), s32[]{:S(2)}) async-start(), calls=%async_computation.5 | async-start | bytes 1966080 | tf_op jit(solution)/shard_map/reduce_scatter | solution.py:409
  235.5 1.0 copy-start.21
  235.6 1.6 copy-start.14
  237.1 0.7 copy-start.25
  237.1 1.7 copy-start.3
  238.9 2.2 copy-start.39
  241.0 3.3 %copy-start.18 = (bf16[320,2048]{1,0:T(8,128)(2,1)S(1)}, bf16[320,2048]{1,0:T(8,128)(2,1)}, u32[]{:S(2)}) copy-start(bf16[320,2048]{1,0:T(8,128)(2,1)} %reshape.293) | copy-start | bytes 3932164
  241.1 3.3 %copy-start.42 = (bf16[320,704]{1,0:T(8,128)(2,1)S(1)}, bf16[320,704]{1,0:T(8,128)(2,1)}, u32[]{:S(2)}) copy-start(bf16[320,704]{1,0:T(8,128)(2,1)} %copy-done.41) | copy-start | bytes 1351684
  246.1 3.1 %copy-start.19 = (bf16[320,2048]{1,0:T(8,128)(2,1)S(1)}, bf16[320,2048]{1,0:T(8,128)(2,1)}, u32[]{:S(2)}) copy-start(bf16[320,2048]{1,0:T(8,128)(2,1)} %reshape.290) | copy-start | bytes 3932164
  246.1 3.1 %copy-start.44 = (f32[320,704]{1,0:T(8,128)S(1)}, f32[320,704]{1,0:T(8,128)}, u32[]{:S(2)}) copy-start(f32[320,704]{1,0:T(8,128)} %fusion.5) | copy-start | bytes 2703364
  246.1 3.0 %copy-start.45 = (f32[320,704]{1,0:T(8,128)S(1)}, f32[320,704]{1,0:T(8,128)}, u32[]{:S(2)}) copy-start(f32[320,704]{1,0:T(8,128)} %fusion.9) | copy-start | bytes 2703364
  249.1 3.4 %copy-start.26 = (bf16[1,512,1,128]{1,3,2,0:T(8,128)(2,1)S(1)}, bf16[1,512,1,128]{1,3,2,0:T(8,128)(2,1)}, u32[]{:S(2)}) copy-start(bf16[1,512,1,128]{1,3,2,0:T(8,128)(2,1)} %copy-done.25) | copy-start | bytes 393220
  249.1 3.4 %copy-start.38 = (bf16[3,2048,128]{2,1,0:T(8,128)(2,1)S(1)}, bf16[3,2048,128]{2,1,0:T(8,128)(2,1)}, u32[]{:S(2)}) copy-start(bf16[3,2048,128]{2,1,0:T(8,128)(2,1)} %param.12) | copy-start | bytes 4718596
  249.2 3.4 %copy-start.40 = (bf16[1,512,1,128]{1,3,2,0:T(8,128)(2,1)S(1)}, bf16[1,512,1,128]{1,3,2,0:T(8,128)(2,1)}, u32[]{:S(2)}) copy-start(bf16[1,512,1,128]{1,3,2,0:T(8,128)(2,1)} %copy-done.39) | copy-start | bytes 393220
  253.8 20.7 %copy-start.5 = (bf16[128,2048]{1,0:T(8,128)(2,1)S(1)}, bf16[128,2048]{1,0:T(8,128)(2,1)}, u32[]{:S(2)}) copy-start(bf16[128,2048]{1,0:T(8,128)(2,1)} %param.10) | copy-start | bytes 1572868
  253.8 20.7 %copy-start.27 = (f32[2048]{0:T(1024)S(1)}, f32[2048]{0:T(1024)}, u32[]{:S(2)}) copy-start(f32[2048]{0:T(1024)} %param.14) | copy-start | bytes 24580
  253.8 20.7 %copy-start.34 = (f32[128]{0:T(128)S(1)}, f32[128]{0:T(128)}, u32[]{:S(2)}) copy-start(f32[128]{0:T(128)} %copy-done.33) | copy-start | bytes 1540
  253.9 21.1 %copy-start.8 = (bf16[128,2048]{1,0:T(8,128)(2,1)S(1)}, bf16[128,2048]{1,0:T(8,128)(2,1)}, u32[]{:S(2)}) copy-start(bf16[128,2048]{1,0:T(8,128)(2,1)} %copy-done.6) | copy-start | bytes 1572868
  253.9 21.1 %copy-start.11 = (bf16[128,2048]{1,0:T(8,128)(2,1)S(1)}, bf16[128,2048]{1,0:T(8,128)(2,1)}, u32[]{:S(2)}) copy-start(bf16[128,2048]{1,0:T(8,128)(2,1)} %param.11) | copy-start | bytes 1572868
  253.9 21.0 %copy-start.32 = (f32[128]{0:T(128)S(1)}, f32[128]{0:T(128)}, u32[]{:S(2)}) copy-start(f32[128]{0:T(128)} %copy-done.30) | copy-start | bytes 1540
  253.9 21.0 %copy-start.36 = (f32[128]{0:T(128)S(1)}, f32[128]{0:T(128)}, u32[]{:S(2)}) copy-start(f32[128]{0:T(128)} %copy-done.35) | copy-start | bytes 1540
  274.9 17.1 %copy-start.1 = (bf16[1,704,2048]{2,1,0:T(8,128)(2,1)S(1)}, bf16[1,704,2048]{2,1,0:T(8,128)(2,1)}, u32[]{:S(2)}) copy-start(bf16[1,704,2048]{2,1,0:T(8,128)(2,1)} %param.17) | copy-start | bytes 8650756
  (2 other events, 1.1 us)
Sparse Core Ops, SparseCore 0:
  233.9 20.0 reduce-scatter.4
  256.3 33.5 reduce-scatter.2

commit v2 on v1

--- a/solution.py
+++ b/solution.py
@@ -1,5 +1,8 @@
+import math
+
 import jax
 import jax.numpy as jnp
+import numpy as np
 from jax import lax
 from jax.experimental import pallas as pl
 from jax.experimental.pallas import tpu as pltpu
@@ -89,7 +92,7 @@
         kernel,
         out_shape=out,
         in_specs=[pl.BlockSpec(memory_space=pltpu.VMEM)] * len(operands),
-        out_specs=pl.BlockSpec(memory_space=pltpu.VMEM),
+        out_specs=jax.tree.map(lambda _: pl.BlockSpec(memory_space=pltpu.VMEM), out),
         scratch_shapes=scratch,
         compiler_params=pltpu.CompilerParams(
             collective_id=collective_id, has_side_effects=True, vmem_limit_bytes=VMEM_LIMIT
@@ -103,16 +106,27 @@
     return me, mate, [lax.rem(me + 2 * j, count) for j in range(1, count // 2)]
 
 
-def gather_head(block, collective_id):
+def gather_head(block, collective_id, routed=None):
     rows, width = block.shape
     count = lax.axis_size("head")
     chunks = 4
     part = rows // chunks
     others = count // 2 - 1
 
-    def kernel(x_ref, o_ref, far_send, far_recv, own_send, own_recv, on_send, on_recv):
+    def kernel(*refs):
+        if routed is None:
+            x_ref, o_ref, far_send, far_recv, own_send, own_recv, on_send, on_recv = refs
+        else:
+            x_ref, o_ref, far_send, far_recv, own_send, own_recv, on_send, on_recv = (
+                refs[0], *refs[routed.inputs + 1 : routed.inputs + 2],
+                *refs[routed.inputs + 3 : routed.inputs + 9]
+            )
+            routed.bind(refs[1 : routed.inputs + 1], refs[routed.inputs + 2], refs[routed.inputs + 9 :])
         me, mate, far = head_peers(count)
-        greet([{"head": mate}] + [{"head": f} for f in far])
+        if routed is None:
+            greet([{"head": mate}] + [{"head": f} for f in far])
+        else:
+            routed.greet()
         sends, passed = [], []
         for c in range(chunks):
             for j, f in enumerate(far):
@@ -123,6 +137,8 @@
         own = remote(x_ref, o_ref.at[span(me, rows)], own_send, own_recv, {"head": mate})
         own.start()
         o_ref[span(me, rows)] = x_ref[...]
+        if routed is not None:
+            routed.start()
         for c in range(chunks):
             for j in range(others):
                 source = lax.rem(me + count - 2 * (j + 1), count)
@@ -139,14 +155,19 @@
                 place = o_ref.at[span(source, rows, c, part)]
                 remote(place, place, on_send.at[j, c], on_recv.at[j, c], {"head": mate}).wait_recv()
         own.wait_send()
+        if routed is not None:
+            routed.finish()
         for copy in sends + passed:
             copy.wait_send()
 
     dma = pltpu.SemaphoreType.DMA
     many = dma((max(others, 1), chunks))
+    out = jax.ShapeDtypeStruct((count * rows, width), block.dtype)
+    scratch = [many, many, dma, dma, many, many]
+    if routed is None:
+        return comm_call(kernel, out, scratch, collective_id, block)
     return comm_call(
-        kernel, jax.ShapeDtypeStruct((count * rows, width), block.dtype),
-        [many, many, dma, dma, many, many], collective_id, block,
+        kernel, (out, routed.out), scratch + routed.scratch, collective_id, block, *routed.operands
     )
 
 
@@ -230,63 +251,245 @@
     )
 
 
-def sum_to_columns(partial, collective_id):
-    groups = lax.axis_size("group")
-    rows, width = partial.shape
-    share = width // groups
-
-    def kernel(p_ref, o_ref, landed, send, recv):
-        group = lax.axis_index("group")
-        rest = [lax.rem(group + k, groups) for k in range(1, groups)]
-        greet([{"group": g} for g in rest])
-        copies = []
-        for k, g in enumerate(rest):
-            copy = remote(p_ref.at[:, span(g, share)], landed.at[k], send.at[k], recv.at[k],
-                          {"group": g})
-            copy.start()
-            copies.append(copy)
-        total = p_ref[:, span(group, share)].astype(jnp.float32)
-        for k, copy in enumerate(copies):
-            copy.wait_recv()
-            total = total + landed[k].astype(jnp.float32)
-        o_ref[...] = total.astype(jnp.bfloat16)
-        for copy in copies:
-            copy.wait_send()
-
-    dma = pltpu.SemaphoreType.DMA((max(groups - 1, 1),))
+class Layout:
+    def __init__(self, slots, width):
+        self.owners = lax.axis_size(("dp", "head"))
+        self.groups = lax.axis_size("group")
+        self.slots, self.width, self.share = slots, width, width // self.groups
+        options = [2**i for i in range(5) if self.share % (128 * 2**i) == 0]
+        padded = {c: -(-slots // (16 // c)) * (16 // c) for c in options}
+        self.cuts = min(options, key=lambda c: (padded[c], c))
+        self.padded = padded[self.cuts]
+        self.slab = self.cuts * self.padded
+        self.piece = self.share // self.cuts
+        self.merged = 16 // math.gcd(slots, 16)
+        while self.owners % self.merged:
+            self.merged //= 2
+        self.blocks = self.owners // self.merged
+        self.block_rows = self.merged * slots
+        unpack = np.zeros((self.cuts, self.block_rows, self.merged * self.slab), np.float32)
+        for c in range(self.cuts):
+            for owner in range(self.merged):
+                for slot in range(slots):
+                    column = owner * self.slab + c * self.padded + slot
+                    unpack[c, owner * slots + slot, column] = 1.0
+        self.unpack = jnp.asarray(unpack, jnp.bfloat16)
+        self.pack = jnp.asarray(unpack.transpose(0, 2, 1), jnp.bfloat16)
+
+    def here(self):
+        heads = lax.axis_size("head")
+        return lax.axis_index("dp") * heads + lax.axis_index("head")
+
+    def peer(self, owner):
+        heads = lax.axis_size("head")
+        return {"dp": owner // heads, "head": lax.rem(owner, heads)}
+
+    def greet(self):
+        barrier = pltpu.get_barrier_semaphore()
+        me, group = self.here(), lax.axis_index("group")
+
+        @pl.loop(1, self.owners)
+        def _(k):
+            peer = self.peer(lax.rem(me + k, self.owners))
+            pl.semaphore_signal(barrier, inc=1, device_id=peer, device_id_type=MESH)
+
+        for k in range(1, self.groups):
+            pl.semaphore_signal(
+                barrier, inc=1, device_id={"group": lax.rem(group + k, self.groups)},
+                device_id_type=MESH,
+            )
+        pl.semaphore_wait(barrier, self.owners - 1 + self.groups - 1)
+
+
+class Routed:
+    def __init__(self, layout, values, picks, scale=None):
+        self.layout = layout
+        self.operands = [values, picks, layout.unpack] + ([] if scale is None else [scale])
+        self.scaled = scale is not None
+        self.inputs = len(self.operands)
+        lay = layout
+        self.out = jax.ShapeDtypeStruct((lay.owners * lay.slots, lay.width), jnp.bfloat16)
+        dma = pltpu.SemaphoreType.DMA
+        over, across = dma((lay.owners,)), dma((max(lay.groups - 1, 1), lay.owners))
+        self.scratch = [
+            pltpu.VMEM((lay.owners * lay.slab, lay.piece), jnp.bfloat16),
+            pltpu.VMEM((lay.groups, lay.owners * lay.slab, lay.piece), jnp.bfloat16),
+            over, over, across, across,
+        ]
+
+    def bind(self, inputs, out, scratch):
+        self.values, self.picks, self.unpack = inputs[:3]
+        self.scale = inputs[3] if self.scaled else None
+        self.got = out
+        self.sent, self.landed, self.over_send, self.over_recv, self.across_send, self.across_recv = scratch
+
+    def greet(self):
+        self.layout.greet()
+
+    def crossing(self, k, j, source, origin):
+        lay, group = self.layout, lax.axis_index("group")
+        place = self.landed.at[origin, span(source, lay.slab)]
+        return remote(place, place, self.across_send.at[j, k], self.across_recv.at[j, k],
+                      {"group": lax.rem(group + j + 1, lay.groups)})
+
+    def start(self):
+        lay = self.layout
+        me, group = lay.here(), lax.axis_index("group")
+        total = jnp.zeros((lay.owners * lay.slab, lay.piece), jnp.float32)
+        for c in range(lay.cuts):
+            columns = self.values[:, span(group, lay.share, c, lay.piece)]
+            total += jnp.dot(self.picks[c], columns, preferred_element_type=jnp.float32)
+        if self.scaled:
+            total = total * self.scale[...]
+        self.sent[...] = total.astype(jnp.bfloat16)
+
+        @pl.loop(1, lay.owners)
+        def _(k):
+            owner = lax.rem(me + k, lay.owners)
+            remote(self.sent.at[span(owner, lay.slab)], self.landed.at[group, span(me, lay.slab)],
+                   self.over_send.at[k], self.over_recv.at[k], lay.peer(owner)).start()
+
+        self.landed[group, span(me, lay.slab)] = self.sent[span(me, lay.slab)]
+        for j in range(lay.groups - 1):
+            self.crossing(0, j, me, group).start()
+
+    def finish(self):
+        lay = self.layout
+        me, group = lay.here(), lax.axis_index("group")
+
+        @pl.loop(1, lay.owners)
+        def _(k):
+            source = lax.rem(me + lay.owners - k, lay.owners)
+            place = self.landed.at[group, span(source, lay.slab)]
+            remote(place, place, self.over_send.at[k], self.over_recv.at[k], lay.peer(source)).wait_recv()
+            for j in range(lay.groups - 1):
+                self.crossing(k, j, source, group).start()
+
+        @pl.loop(0, lay.owners)
+        def _(k):
+            source = lax.rem(me + lay.owners - k, lay.owners)
+            for j in range(lay.groups - 1):
+                origin = lax.rem(group + lay.groups - j - 1, lay.groups)
+                self.crossing(k, j, source, origin).wait_recv()
+
+        wide = lay.merged * lay.slab
+        for g in range(lay.groups):
+            for b in range(lay.blocks):
+                block = self.landed[g, b * wide : (b + 1) * wide]
+                for c in range(lay.cuts):
+                    at = g * lay.share + c * lay.piece
+                    self.got[b * lay.block_rows : (b + 1) * lay.block_rows, at : at + lay.piece] = jnp.dot(
+                        self.unpack[c], block, preferred_element_type=jnp.float32
+                    ).astype(jnp.bfloat16)
+
+        @pl.loop(0, lay.owners)
+        def _(k):
+            owner = lax.rem(me + k, lay.owners)
+            source = lax.rem(me + lay.owners - k, lay.owners)
+            for j in range(lay.groups - 1):
+                self.crossing(k, j, source, group).wait_send()
+
+            @pl.when(k > 0)
+            def _():
+                place = self.sent.at[span(owner, lay.slab)]
+                remote(place, place, self.over_send.at[k], self.over_recv.at[k],
+                       lay.peer(owner)).wait_send()
+
+
+def route(routed, collective_id):
+    def kernel(*refs):
+        routed.bind(refs[: routed.inputs], refs[routed.inputs], refs[routed.inputs + 1 :])
+        routed.greet()
+        routed.start()
+        routed.finish()
+
+    return comm_call(kernel, routed.out, routed.scratch, collective_id, *routed.operands)
+
+
+def route_back(lay, partial, takes, collective_id):
+    rows = takes.shape[1]
+    others = max(lay.groups - 1, 1)
+    wide = lay.merged * lay.slab
+
+    def kernel(p_ref, pack_ref, take_ref, o_ref, landed, sent, back,
+               sum_send, sum_recv, over_send, over_recv, across_send, across_recv):
+        me, group = lay.here(), lax.axis_index("group")
+        rest = [lax.rem(group + k, lay.groups) for k in range(1, lay.groups)]
+        first = me // lay.merged
+        lay.greet()
+
+        def summing(b, k):
+            at = span(lax.rem(first + b + 1, lay.blocks), lay.block_rows)
+            return remote(p_ref.at[at, span(rest[k], lay.share)], landed.at[k, at],
+                          sum_send.at[k, b], sum_recv.at[k, b], {"group": rest[k]})
+
+        for b in range(lay.blocks):
+            for k in range(lay.groups - 1):
+                summing(b, k).start()
+        for b in range(lay.blocks):
+            block = lax.rem(first + b + 1, lay.blocks)
+            at = span(block, lay.block_rows)
+            total = p_ref[at, span(group, lay.share)].astype(jnp.float32)
+            for k in range(lay.groups - 1):
+                summing(b, k).wait_recv()
+                total = total + landed[k, at].astype(jnp.float32)
+            total = total.astype(jnp.bfloat16)
+            packed = jnp.zeros((wide, lay.piece), jnp.float32)
+            for c in range(lay.cuts):
+                packed += jnp.dot(pack_ref[c], total[:, c * lay.piece : (c + 1) * lay.piece],
+                                  preferred_element_type=jnp.float32)
+            sent[span(block, wide)] = packed.astype(jnp.bfloat16)
+
+            @pl.loop(0, lay.merged)
+            def _(j):
+                owner = block * lay.merged + j
+
+                @pl.when(owner != me)
+                def _():
+                    remote(sent.at[span(owner, lay.slab)], back.at[span(me, lay.slab)],
+                           over_send.at[owner], over_recv.at[me], lay.peer(owner)).start()
+
+        back[span(me, lay.slab)] = sent[span(me, lay.slab)]
+
+        @pl.loop(1, lay.owners)
+        def _(k):
+            source = lax.rem(me + k, lay.owners)
+            place = back.at[span(source, lay.slab)]
+            remote(place, place, over_send.at[source], over_recv.at[source],
+                   lay.peer(source)).wait_recv()
+
+        for c in range(lay.cuts):
+            o_ref[:, span(group, lay.share, c, lay.piece)] = jnp.dot(
+                take_ref[c], back[...], preferred_element_type=jnp.float32
+            ).astype(jnp.bfloat16)
+        mine = o_ref.at[:, span(group, lay.share)]
+        for k in range(lay.groups - 1):
+            remote(mine, mine, across_send.at[k], across_recv.at[k], {"group": rest[k]}).start()
+        for k in range(lay.groups - 1):
+            origin = lax.rem(group + lay.groups - k - 1, lay.groups)
+            place = o_ref.at[:, span(origin, lay.share)]
+            remote(place, place, across_send.at[k], across_recv.at[k], {"group": rest[k]}).wait_recv()
+        for k in range(lay.groups - 1):
+            remote(mine, mine, across_send.at[k], across_recv.at[k], {"group": rest[k]}).wait_send()
+            for b in range(lay.blocks):
+                summing(b, k).wait_send()
+
+        @pl.loop(1, lay.owners)
+        def _(k):
+            owner = lax.rem(me + k, lay.owners)
+            place = sent.at[span(owner, lay.slab)]
+            remote(place, place, over_send.at[owner], over_recv.at[owner], lay.peer(owner)).wait_send()
+
+    dma = pltpu.SemaphoreType.DMA
+    b16 = jnp.bfloat16
     return comm_call(
-        kernel, jax.ShapeDtypeStruct((rows, share), jnp.bfloat16),
-        [pltpu.VMEM((max(groups - 1, 1), rows, share), jnp.bfloat16), dma, dma],
-        collective_id, partial,
-    )
-
-
-def gather_columns(block, collective_id):
-    groups = lax.axis_size("group")
-    rows, share = block.shape
-
-    def kernel(x_ref, o_ref, send, recv):
-        group = lax.axis_index("group")
-        rest = [lax.rem(group + k, groups) for k in range(1, groups)]
-        greet([{"group": g} for g in rest])
-        copies = []
-        for k, g in enumerate(rest):
-            copy = remote(x_ref, o_ref.at[:, span(group, share)], send.at[k], recv.at[k],
-                          {"group": g})
-            copy.start()
-            copies.append(copy)
-        o_ref[:, span(group, share)] = x_ref[...]
-        for k in range(groups - 1):
-            source = lax.rem(group + groups - k - 1, groups)
-            place = o_ref.at[:, span(source, share)]
-            remote(place, place, send.at[k], recv.at[k], {"group": rest[k]}).wait_recv()
-        for copy in copies:
-            copy.wait_send()
-
-    dma = pltpu.SemaphoreType.DMA((max(groups - 1, 1),))
-    return comm_call(
-        kernel, jax.ShapeDtypeStruct((rows, groups * share), block.dtype), [dma, dma],
-        collective_id, block,
+        kernel, jax.ShapeDtypeStruct((rows, lay.width), b16),
+        [pltpu.VMEM((others, lay.owners * lay.slots, lay.share), b16),
+         pltpu.VMEM((lay.owners * lay.slab, lay.piece), b16),
+         pltpu.VMEM((lay.owners * lay.slab, lay.piece), b16),
+         dma((others, lay.blocks)), dma((others, lay.blocks)),
+         dma((lay.owners,)), dma((lay.owners,)), dma((others,)), dma((others,))],
+        collective_id, partial, lay.pack, takes,
     )
 
 
@@ -300,7 +503,35 @@
     tokens_f = tokens.astype(jnp.float32)
     scale_one = inverse_rms(tokens_f)
     normed_one = (tokens_f * scale_one * gain_attn).astype(jnp.bfloat16)
-    shard_rows = gather_head(normed_one, 0)
+    top_count = expert_ids.shape[1]
+    owners = lax.axis_size(("dp", "head"))
+    local_count = w_gate_up.shape[0]
+    expert_count = local_count * owners
+    capacity = max(row_count * top_count * 5 // (4 * expert_count), 2)
+    flat_ids = expert_ids.reshape(-1)
+    onehot = (flat_ids[:, None] == lax.iota(jnp.int32, expert_count)[None, :]).astype(jnp.int32)
+    earlier = jnp.cumsum(onehot, axis=0) - onehot
+    slot_ids = jnp.sum(onehot * earlier, axis=1)
+    slots = local_count * capacity
+    lay = Layout(slots, width)
+    owner_ids = flat_ids // local_count
+    places = owner_ids * lay.slab + (flat_ids % local_count) * capacity + slot_ids
+    slab_rows = owners * lay.slab
+    row_ids = lax.iota(jnp.int32, slab_rows)
+    cut_ids = row_ids % lay.slab // lay.padded
+    plain_ids = row_ids - cut_ids * lay.padded
+    places = places.reshape(row_count, top_count)
+    matches = plain_ids[:, None, None] == places[None]
+    row_gates = jnp.sum(jnp.where(matches, gates[None], 0.0), axis=(1, 2))[:, None]
+    cuts = lax.iota(jnp.int32, lay.cuts)
+    picks = (
+        jnp.any(matches, axis=2)[None] & (cut_ids[None, :] == cuts[:, None])[:, :, None]
+    ).astype(jnp.bfloat16)
+    takes = (
+        jnp.any(places[:, :, None] == plain_ids[None, None, :], axis=1)[None]
+        & (cut_ids[None, :] == cuts[:, None])[:, None, :]
+    ).astype(jnp.bfloat16)
+    shard_rows, got_grads = gather_head(normed_one, 0, Routed(lay, grad_out, picks, row_gates))
     fresh = jnp.einsum("rd,idh->irh", shard_rows, w_qkv, preferred_element_type=jnp.float32).astype(
         jnp.bfloat16
     )
@@ -326,53 +557,17 @@
     scale_two = inverse_rms(hidden_f)
     normed_two = (hidden_f * scale_two * gain_ffn).astype(jnp.bfloat16)
     grad_f = grad_out.astype(jnp.float32)
-    top_count = expert_ids.shape[1]
-    owners = lax.axis_size(("dp", "head"))
-    local_count = w_gate_up.shape[0]
-    expert_count = local_count * owners
-    capacity = max(row_count * top_count * 5 // (4 * expert_count), 2)
-    flat_ids = expert_ids.reshape(-1)
-    onehot = (flat_ids[:, None] == lax.iota(jnp.int32, expert_count)[None, :]).astype(jnp.int32)
-    earlier = jnp.cumsum(onehot, axis=0) - onehot
-    slot_ids = jnp.sum(onehot * earlier, axis=1)
-    targets = flat_ids * capacity + slot_ids
-    matches = (lax.iota(jnp.int32, expert_count * capacity)[:, None] == targets[None, :]).reshape(
-        expert_count * capacity, row_count, top_count
-    )
-    picker = jnp.any(matches, axis=2).astype(jnp.bfloat16)
-    weigher = jnp.sum(jnp.where(matches, gates[None, :, :], 0.0), axis=2)
-    send_rows = (
-        jnp.dot(picker, normed_two, preferred_element_type=jnp.float32)
-        .astype(jnp.bfloat16)
-        .reshape(expert_count, capacity, width)
-    )
-    send_grads = (
-        jnp.dot(
-            weigher, grad_f, precision=lax.Precision.HIGHEST, preferred_element_type=jnp.float32
-        )
-        .astype(jnp.bfloat16)
-        .reshape(expert_count, capacity, width)
-    )
-    got_rows, got_grads = (
-        lax.all_to_all(send_rows, ("dp", "head"), split_axis=0, concat_axis=1, tiled=True),
-        lax.all_to_all(send_grads, ("dp", "head"), split_axis=0, concat_axis=1, tiled=True),
-    )
+    got_rows = route(Routed(lay, normed_two, picks), 2)
+
+    def by_expert(got):
+        got = got.reshape(owners, local_count, capacity, width)
+        return jnp.swapaxes(got, 0, 1).reshape(local_count, owners * capacity, width)
+
+    got_rows, got_grads = by_expert(got_rows), by_expert(got_grads)
     grad_pair, grad_down, returned = expert_work(got_rows, got_grads, w_gate_up, w_down)
-    shared = sum_to_columns(
-        returned.astype(jnp.bfloat16).reshape(expert_count * capacity, width), 2
-    ).reshape(local_count, owners * capacity, -1)
-    back_half = lax.all_to_all(
-        shared, ("dp", "head"), split_axis=1, concat_axis=0, tiled=True
-    )
-    grad_normed = gather_columns(
-        jnp.einsum(
-            "cr,cd->rd",
-            picker,
-            back_half.reshape(expert_count * capacity, -1),
-            preferred_element_type=jnp.float32,
-        ).astype(jnp.bfloat16),
-        3,
-    ).astype(jnp.float32)
+    returned = returned.astype(jnp.bfloat16).reshape(local_count, owners, capacity, width)
+    returned = jnp.swapaxes(returned, 0, 1).reshape(owners * slots, width)
+    grad_normed = route_back(lay, returned, takes, 3).astype(jnp.float32)
     grad_hidden = grad_f + norm_backward(hidden_f, scale_two, gain_ffn, grad_normed)
     grad_hidden_b = grad_hidden.astype(jnp.bfloat16)
     shard_rows = gather_head(grad_hidden_b, 4)

time: 300 us -> 243 us (0.81)
  Pallas kernels: 99 us -> 165 us
  waiting for transfers between devices: 57.8 us -> 11.6 us
  blocking collectives: 26.7 us -> 0 us
  local copies, waits for them, and re-layouts: 25.5 us -> 8.24 us
  matrix products: 42.8 us -> 27.8 us
  starting transfers between devices: 15.1 us -> 0.3 us
    pallas_call x6, Pallas kernels: 99 us -> 165 us  [comm_call(): pl.pallas_call(kernel, out_shape=out, in_specs=[pl.BlockSpec(memory_space...]
    all_to_all x2 -> x0, waiting for transfers between devices: 45.8 us -> none  [the longest x1 25.8 us: body(): lax.all_to_all(send_rows, ('dp', 'head'), split_axis=0, concat_axis=1, ti...]
    all_to_all x1 -> x0, blocking collectives: 26.7 us -> none  [body(): lax.all_to_all(shared, ('dp', 'head'), split_axis=1, concat_axis=0, tiled...]
    all_to_all x2 -> x0, starting transfers between devices: 14.8 us -> none  [the longest x1 9.15 us: body(): lax.all_to_all(send_grads, ('dp', 'head'), split_axis=0, concat_axis=1, t...]
    reshape x3 -> x0, local copies, waits for them, and re-layouts: 7.41 us -> none  [the longest x1 3.21 us: body(): send_grads = jnp.dot(weigher, grad_f, precision=lax.Precision.HIGHEST, pr...]
    another operation x3 -> x1, local copies, waits for them, and re-layouts: 6.58 us -> 0.01 us
    dot_general x3 -> x0, matrix products: 5.62 us -> none  [the longest x1 2.26 us: body(): jnp.dot(weigher, grad_f, precision=lax.Precision.HIGHEST, preferred_eleme...]
    unnamed x1, other arithmetic: 4.47 us -> 0.01 us
  transfers between devices with their start and end apart: 4 -> 2, of which waited for: 3 -> 1; matrix products, arithmetic and copies ran while one was open for 13% -> 9% of each run, Pallas kernels for 7% -> 9%
where the time goes in v2:
time: 243 us
  Pallas kernels  165 us (68%)
  matrix products  27.8 us (11%)
  other arithmetic  14.9 us (6%)
  between operations  14.8 us (6%)
  waiting for transfers between devices  11.6 us (5%)
  local copies, waits for them, and re-layouts  8.24 us (3%)
    pallas_call x6, Pallas kernels, comm_call(): pl.pallas_call(kernel, out_shape=out, in_specs=[pl.BlockSpec(memory_space...  165 us
    reduce_scatter x1, waiting for transfers between devices, body(): lax.psum_scatter(grad_proj.astype(jnp.bfloat16), 'dp', scatter_dimension=...  11.6 us
    unnamed x86, local copies, waits for them, and re-layouts  7.35 us
  transfers between devices with their start and end apart: 2, of which 1 were waited for; matrix products, arithmetic and copies ran while one was open for 9% of the time, Pallas kernels for 9%

profile of v2, /device:TPU:0, one launch (start us, length us, event | category | flops | bytes accessed | tf_op | source)
XLA Modules:
  0.0 242.6 jit_solution(12115207589974868519)
XLA Ops:
  7.3 0.9 copy.41
  8.5 0.6 reduce-window.6
  9.6 0.8 multiply_add_fusion
  10.8 1.2 fusion.57
  12.1 1.1 fusion.34
  13.4 1.2 fusion.51.refs_0_
  14.7 1.0 and_convert_fusion.1.refs_2_.refs_1_
  15.7 44.2 %shard_map.155 = (bf16[512,2048]{1,0:T(8,128)(2,1)}, bf16[320,2048]{1,0:T(8,128)(2,1)S(1)}) custom-call(bf16[128,2048]{1,0:T(8,128)(2,1)S(1)} %fusion.51.refs_0_, bf16[128,2048]{1,0:T(8,128)(2,1)S(1)} %copy-done.2, bf16[4,1280,128]{2,1,0:T(8,128)(2,1)S(1)} %and_convert_fusion.1.refs_2_.refs_1_, bf16[4,80,320]{2,1,0:T(8,128)(2,1)S(1)} %copy-done.7, ...), custom_call_target="tpu_custom_call" | custom-call | tf_op jit(solution)/shard_map/pallas_call | solution.py:91
  60.0 3.3 %fusion.38 = bf16[3,512,128]{2,1,0:T(8,128)(2,1)S(1)} fusion(bf16[3,2048,128]{2,1,0:T(8,128)(2,1)S(1)} %copy-done.30, bf16[512,2048]{1,0:T(8,128)(2,1)} %get-tuple-element.7), kind=kOutput, calls=%fused_computation.51 | convolution fusion | flops 805502976 | bytes 4063232 | tf_op jit(solution)/shard_map/rd,idh->irh/dot_general | solution.py:535
  63.3 0.3 fusion.86
  64.0 0.6 copy-done.15
  64.6 0.3 fusion.41
  64.9 0.7 copy-done.17
  65.6 0.7 convolution_convert_fusion.3.p_ref
  66.4 21.6 %shard_map.156 = f32[128,2048]{1,0:T(8,128)S(1)} custom-call(bf16[512,2048]{1,0:T(8,128)(2,1)S(1)} %convolution_convert_fusion.3.p_ref), custom_call_target="tpu_custom_call" | custom-call | tf_op jit(solution)/shard_map/pallas_call | solution.py:91
  88.5 28.0 %shard_map.157 = bf16[320,2048]{1,0:T(8,128)(2,1)S(1)} custom-call(bf16[128,2048]{1,0:T(8,128)(2,1)S(1)} %fusion.45.refs_0_, bf16[4,1280,128]{2,1,0:T(8,128)(2,1)S(1)} %and_convert_fusion.1.refs_2_.refs_1_, bf16[4,80,320]{2,1,0:T(8,128)(2,1)S(1)} %copy-done.7), custom_call_target="tpu_custom_call" | custom-call | tf_op jit(solution)/shard_map/pallas_call | solution.py:91
  116.5 1.2 fusion.5
  117.8 1.2 fusion.9
  119.3 1.5 multiply_convert_fusion.2
  120.8 1.2 fusion.3
  122.1 1.2 fusion.16.p_ref
  123.3 35.1 %shard_map.158 = bf16[128,2048]{1,0:T(8,128)(2,1)S(1)} custom-call(bf16[320,2048]{1,0:T(8,128)(2,1)S(1)} %fusion.16.p_ref, bf16[4,320,80]{2,1,0:T(8,128)(2,1)S(1)} %copy-done.8, bf16[4,128,1280]{2,1,0:T(8,128)(2,1)S(1)} %and_convert_fusion.take_ref), custom_call_target="tpu_custom_call" | custom-call | tf_op jit(solution)/shard_map/pallas_call | solution.py:91
  158.4 0.3 fusion.46
  158.8 0.4 fusion.66.refs_0_
  159.2 15.4 %shard_map.159 = bf16[512,2048]{1,0:T(8,128)(2,1)S(1)} custom-call(bf16[128,2048]{1,0:T(8,128)(2,1)S(1)} %fusion.66.refs_0_), custom_call_target="tpu_custom_call" | custom-call | tf_op jit(solution)/shard_map/pallas_call | solution.py:91
  174.7 1.3 copy-done.1
  176.0 1.2 convolution_convert_fusion.5
  177.2 0.3 reduce-scatter.3.cloned.1.call-start
  177.5 2.5 %convolution_convert_fusion.9 = bf16[512,128]{1,0:T(8,128)(2,1)S(1)} fusion(bf16[512,2048]{1,0:T(8,128)(2,1)} %copy-done.1, bf16[128,2048]{1,0:T(8,128)(2,1)} %param.15), kind=kOutput, calls=%fused_computation.55 | convolution fusion | flops 268500992 | bytes 2752512 | tf_op jit(solution)/shard_map/rd,hd->rh/dot_general | solution.py:575
  180.1 0.3 multiply_reduce_fusion
  180.4 0.3 multiply_convert_fusion
  180.7 0.3 fusion.43
  181.3 0.3 fusion.44
  181.6 0.3 copy-done.21
  181.9 0.7 copy-done.31
  182.6 0.5 copy-done.29
  183.0 2.1 fusion.19
  185.2 2.9 %bitcast_convert_fusion.p_ref = bf16[512,2048]{1,0:T(8,128)(2,1)S(1)} fusion(bf16[3,2048,128]{2,1,0:T(8,128)(2,1)} %param.14, bf16[1,512,1,128]{1,3,2,0:T(8,128)(2,1)} %copy-done.31, bf16[1,512,1,128]{1,3,2,0:T(8,128)(2,1)S(1)} %fusion.43, bf16[1,512,1,128]{1,3,2,0:T(8,128)(2,1)} %copy-done.21), kind=kOutput, calls=%fused_computation.1 | convolution fusion | flops 806748160 | bytes 4063232 | tf_op jit(solution)/shard_map/irh,idh->rd/dot_general | solution.py:598
  188.1 20.7 %shard_map.160 = f32[128,2048]{1,0:T(8,128)S(1)} custom-call(bf16[512,2048]{1,0:T(8,128)(2,1)S(1)} %bitcast_convert_fusion.p_ref), custom_call_target="tpu_custom_call" | custom-call | tf_op jit(solution)/shard_map/pallas_call | solution.py:91
  208.8 0.3 fusion.52
  209.2 1.7 fusion.1
  210.9 1.7 fusion
  212.6 3.0 %pad_maximum_fusion = bf16[1,2,2048,704]{2,3,1,0:T(8,128)(2,1)} fusion(bf16[1,1,2048,704]{2,3,1,0:T(8,128)(2,1)S(1)} %fusion.1, bf16[1,1,2048,704]{2,3,1,0:T(8,128)(2,1)S(1)} %fusion), kind=kLoop, calls=%fused_computation | loop fusion | flops 2883584 | bytes 11534336 | tf_op jit(solution)/shard_map/stack | solution.py:57
  215.7 3.4 %fusion.2 = bf16[1,704,2048]{2,1,0:T(8,128)(2,1)} fusion(bf16[320,2048]{1,0:T(8,128)(2,1)S(1)} %copy-done.10, f32[320,704]{1,0:T(8,128)S(1)} %copy-done.39, f32[320,704]{1,0:T(8,128)S(1)} %copy-done.37), kind=kOutput, calls=%fused_computation.8 | convolution fusion | flops 925540352 | bytes 5996544 | tf_op jit(solution)/shard_map/esf,esd->efd/dot_general | solution.py:52
  219.1 1.4 fusion.56
  220.5 1.6 convert_element_type.184
  222.1 11.6 %reduce-scatter.3.cloned.1.call-done = bf16[3,512,128]{1,2,0:T(8,128)(2,1)} async-done(((bf16[3,2048,128]{1,2,0:T(8,128)(2,1)}), bf16[3,512,128]{1,2,0:T(8,128)(2,1)}) %reduce-scatter.3.cloned.1.call-update) | async-done | bytes 393232 | tf_op jit(solution)/shard_map/reduce_scatter | solution.py:604
  233.7 2.0 copy.47
  (107 shorter events, 3.1 us)
Async XLA Ops:
  7.2 112.1 %copy-start = (bf16[1,704,2048]{2,1,0:T(8,128)(2,1)S(1)}, bf16[1,704,2048]{2,1,0:T(8,128)(2,1)}, u32[]{:S(2)}) copy-start(bf16[1,704,2048]{2,1,0:T(8,128)(2,1)} %param.19) | copy-start | bytes 8650756
  7.2 213.3 %reduce-scatter.5.cloned.1.call-start = ((), (), s32[]{:S(2)}) async-start(), calls=%async_computation.3 | async-start | bytes 655360 | tf_op jit(solution)/shard_map/reduce_scatter | solution.py:607
  9.6 6.2 %copy-start.2 = (bf16[128,2048]{1,0:T(8,128)(2,1)S(1)}, bf16[128,2048]{1,0:T(8,128)(2,1)}, u32[]{:S(2)}) copy-start(bf16[128,2048]{1,0:T(8,128)(2,1)} %refs_1_.1) | copy-start | bytes 1572868
  9.6 6.1 %copy-start.7 = (bf16[4,80,320]{2,1,0:T(8,128)(2,1)S(1)}, bf16[4,80,320]{2,1,0:T(8,128)(2,1)}, u32[]{:S(2)}) copy-start(bf16[4,80,320]{2,1,0:T(8,128)(2,1)} %constant.80.clone.refs_3_.refs_2_) | copy-start | bytes 614404
  12.1 47.9 %copy-start.25 = (f32[128]{0:T(128)}, f32[128]{0:T(128)S(1)}, u32[]{:S(2)}) copy-start(f32[128]{0:T(128)S(1)} %add_rsqrt_fusion.1) | copy-start | bytes 1540
  14.7 45.3 %copy-start.30 = (bf16[3,2048,128]{2,1,0:T(8,128)(2,1)S(1)}, bf16[3,2048,128]{2,1,0:T(8,128)(2,1)}, u32[]{:S(2)}) copy-start(bf16[3,2048,128]{2,1,0:T(8,128)(2,1)} %param.14) | copy-start | bytes 4718596
  59.9 59.3 %copy-start.9 = (bf16[320,2048]{1,0:T(8,128)(2,1)}, bf16[320,2048]{1,0:T(8,128)(2,1)S(1)}, u32[]{:S(2)}) copy-start(bf16[320,2048]{1,0:T(8,128)(2,1)S(1)} %get-tuple-element.8) | copy-start | bytes 3932164
  63.3 0.7 copy-start.18
  63.6 1.0 copy-start.15
  64.6 1.0 copy-start.17
  64.6 51.9 %slice-start = ((s8[5767168]{0:T(1024)(128)(4,1)}), s8[4194304]{0:T(1024)(128)(4,1)S(1)}, s32[]{:S(2)}) async-start(s8[5767168]{0:T(1024)(128)(4,1)} %bitcast.127), calls=%async_computation.4 | async-start | bytes 8388608
  66.4 21.7 %copy-start.11 = (bf16[128,2048]{1,0:T(8,128)(2,1)S(1)}, bf16[128,2048]{1,0:T(8,128)(2,1)}, u32[]{:S(2)}) copy-start(bf16[128,2048]{1,0:T(8,128)(2,1)} %param.12) | copy-start | bytes 1572868
  66.4 21.9 %copy-start.20 = (f32[2048]{0:T(1024)S(1)}, f32[2048]{0:T(1024)}, u32[]{:S(2)}) copy-start(f32[2048]{0:T(1024)} %param.17) | copy-start | bytes 24580
  66.4 50.1 %slice-start.1 = ((s8[5767168]{0:T(1024)(128)(4,1)}), s8[1572864]{0:T(1024)(128)(4,1)S(1)}, s32[]{:S(2)}) async-start(s8[5767168]{0:T(1024)(128)(4,1)} %bitcast.127), calls=%async_computation.5 | async-start | bytes 3145728
  88.3 70.5 %copy-start.13 = (bf16[128,2048]{1,0:T(8,128)(2,1)}, bf16[128,2048]{1,0:T(8,128)(2,1)S(1)}, u32[]{:S(2)}) copy-start(bf16[128,2048]{1,0:T(8,128)(2,1)S(1)} %get-tuple-element.30) | copy-start | bytes 1572868
  88.3 70.5 %copy-start.23 = (f32[128]{0:T(128)}, f32[128]{0:T(128)S(1)}, u32[]{:S(2)}) copy-start(f32[128]{0:T(128)S(1)} %add_rsqrt_fusion) | copy-start | bytes 1540
  116.5 1.2 copy-start.5
  117.8 1.5 copy-start.36
  119.0 1.8 copy-start.38
  120.8 1.2 copy-start.32
  120.8 1.2 copy-start.34
  122.0 1.3 copy-start.8
  123.3 35.5 %copy-start.3 = (bf16[128,2048]{1,0:T(8,128)(2,1)S(1)}, bf16[128,2048]{1,0:T(8,128)(2,1)}, u32[]{:S(2)}) copy-start(bf16[128,2048]{1,0:T(8,128)(2,1)} %refs_1_.1) | copy-start | bytes 1572868
  158.8 15.8 %copy-start.27 = (f32[128]{0:T(128)}, f32[128]{0:T(128)S(1)}, u32[]{:S(2)}) copy-start(f32[128]{0:T(128)S(1)} %broadcast_multiply_fusion.1) | copy-start | bytes 1540
  174.6 1.3 copy-start.1
  177.2 56.5 %reduce-scatter.3.cloned.1.call-start = ((), (), s32[]{:S(2)}) async-start(), calls=%async_computation.2 | async-start | bytes 1966080 | tf_op jit(solution)/shard_map/reduce_scatter | solution.py:604
  177.5 2.5 %copy-start.16 = (f32[512,512]{0,1:T(8,128)S(1)}, f32[512,512]{0,1:T(8,128)}, u32[]{:S(2)}) copy-start(f32[512,512]{0,1:T(8,128)} %copy-done.15) | copy-start | bytes 3145732
  177.5 2.5 %copy-start.19 = (bf16[3,512,128]{2,1,0:T(8,128)(2,1)S(1)}, bf16[3,512,128]{2,1,0:T(8,128)(2,1)}, u32[]{:S(2)}) copy-start(bf16[3,512,128]{2,1,0:T(8,128)(2,1)} %copy-done.18) | copy-start | bytes 1179652
  181.2 0.7 copy-start.21
  181.3 1.8 copy-start.29
  181.9 0.7 copy-start.31
  188.1 20.7 %copy-start.12 = (bf16[128,2048]{1,0:T(8,128)(2,1)S(1)}, bf16[128,2048]{1,0:T(8,128)(2,1)}, u32[]{:S(2)}) copy-start(bf16[128,2048]{1,0:T(8,128)(2,1)} %param.12) | copy-start | bytes 1572868
  188.1 20.7 %copy-start.22 = (f32[2048]{0:T(1024)S(1)}, f32[2048]{0:T(1024)}, u32[]{:S(2)}) copy-start(f32[2048]{0:T(1024)} %param.16) | copy-start | bytes 24580
  188.1 20.7 %copy-start.26 = (f32[128]{0:T(128)S(1)}, f32[128]{0:T(128)}, u32[]{:S(2)}) copy-start(f32[128]{0:T(128)} %copy-done.25) | copy-start | bytes 1540
  188.1 21.0 %copy-start.6 = (bf16[320,2048]{1,0:T(8,128)(2,1)S(1)}, bf16[320,2048]{1,0:T(8,128)(2,1)}, u32[]{:S(2)}) copy-start(bf16[320,2048]{1,0:T(8,128)(2,1)} %copy-done.5) | copy-start | bytes 3932164
  188.1 21.0 %copy-start.35 = (bf16[320,704]{1,0:T(8,128)(2,1)S(1)}, bf16[320,704]{1,0:T(8,128)(2,1)}, u32[]{:S(2)}) copy-start(bf16[320,704]{1,0:T(8,128)(2,1)} %copy-done.34) | copy-start | bytes 1351684
  209.1 1.7 copy-start.33
  212.6 3.1 %copy-start.10 = (bf16[320,2048]{1,0:T(8,128)(2,1)S(1)}, bf16[320,2048]{1,0:T(8,128)(2,1)}, u32[]{:S(2)}) copy-start(bf16[320,2048]{1,0:T(8,128)(2,1)} %copy-done.9) | copy-start | bytes 3932164
  212.6 3.1 %copy-start.37 = (f32[320,704]{1,0:T(8,128)S(1)}, f32[320,704]{1,0:T(8,128)}, u32[]{:S(2)}) copy-start(f32[320,704]{1,0:T(8,128)} %copy-done.36) | copy-start | bytes 2703364
  212.6 3.0 %copy-start.39 = (f32[320,704]{1,0:T(8,128)S(1)}, f32[320,704]{1,0:T(8,128)}, u32[]{:S(2)}) copy-start(f32[320,704]{1,0:T(8,128)} %copy-done.38) | copy-start | bytes 2703364
  215.7 3.4 %copy-start.4 = (bf16[128,2048]{1,0:T(8,128)(2,1)S(1)}, bf16[128,2048]{1,0:T(8,128)(2,1)}, u32[]{:S(2)}) copy-start(bf16[128,2048]{1,0:T(8,128)(2,1)} %refs_1_.1) | copy-start | bytes 1572868
  215.7 3.4 %copy-start.14 = (bf16[128,2048]{1,0:T(8,128)(2,1)S(1)}, bf16[128,2048]{1,0:T(8,128)(2,1)}, u32[]{:S(2)}) copy-start(bf16[128,2048]{1,0:T(8,128)(2,1)} %copy-done.13) | copy-start | bytes 1572868
  215.7 3.4 %copy-start.24 = (f32[128]{0:T(128)S(1)}, f32[128]{0:T(128)}, u32[]{:S(2)}) copy-start(f32[128]{0:T(128)} %copy-done.23) | copy-start | bytes 1540
  215.7 3.4 %copy-start.28 = (f32[128]{0:T(128)S(1)}, f32[128]{0:T(128)}, u32[]{:S(2)}) copy-start(f32[128]{0:T(128)} %copy-done.27) | copy-start | bytes 1540
Sparse Core Ops, SparseCore 0:
  177.4 20.5 reduce-scatter.4
  200.2 33.4 reduce-scatter.2

commit v3 on v2

--- a/solution.py
+++ b/solution.py
@@ -128,6 +128,8 @@
         else:
             routed.greet()
         sends, passed = [], []
+        if routed is not None:
+            routed.start()
         for c in range(chunks):
             for j, f in enumerate(far):
                 copy = remote(x_ref.at[pl.ds(c * part, part)], o_ref.at[span(me, rows, c, part)],
@@ -137,9 +139,9 @@
         own = remote(x_ref, o_ref.at[span(me, rows)], own_send, own_recv, {"head": mate})
         own.start()
         o_ref[span(me, rows)] = x_ref[...]
-        if routed is not None:
-            routed.start()
-        for c in range(chunks):
+        for c in range(chunks):
+            if routed is not None:
+                routed.forward(c, chunks)
             for j in range(others):
                 source = lax.rem(me + count - 2 * (j + 1), count)
                 place = o_ref.at[span(source, rows, c, part)]
@@ -171,10 +173,84 @@
     )
 
 
+def gather_head_split(block, collective_id):
+    rows, width = block.shape
+    count, groups = lax.axis_size("head"), lax.axis_size("group")
+    part = 16
+    chunks = rows // (part * groups)
+    share = part * chunks
+    others = count // 2 - 1
+
+    def kernel(x_ref, o_ref, far_send, far_recv, own_send, own_recv,
+               across_send, across_recv, on_send, on_recv):
+        me, mate, far = head_peers(count)
+        group = lax.axis_index("group")
+        rest = [lax.rem(group + k, groups) for k in range(1, groups)]
+        greet([{"head": mate}] + [{"head": f} for f in far] + [{"group": g} for g in rest])
+        copies = []
+
+        def place(block, owner_group, c):
+            start = pl.multiple_of(block * rows + owner_group * share + c * part, part)
+            return o_ref.at[pl.ds(start, part)]
+
+        for c in range(chunks):
+            for j, f in enumerate(far):
+                copy = remote(x_ref.at[span(group, share, c, part)], place(me, group, c),
+                              far_send.at[j, c], far_recv.at[j, c], {"head": f})
+                copy.start()
+                copies.append(copy)
+        own = remote(x_ref, o_ref.at[span(me, rows)], own_send, own_recv, {"head": mate})
+        own.start()
+        o_ref[span(me, rows)] = x_ref[...]
+
+        def pass_on(j, k, c, at):
+            copy = remote(at, at, on_send.at[j, k, c], on_recv.at[j, k, c], {"head": mate})
+            copy.start()
+            copies.append(copy)
+
+        for c in range(chunks):
+            for j in range(others):
+                at = place(lax.rem(me + count - 2 * (j + 1), count), group, c)
+                remote(at, at, far_send.at[j, c], far_recv.at[j, c], {"head": mate}).wait_recv()
+                for k, g in enumerate(rest):
+                    copy = remote(at, at, across_send.at[j, k, c], across_recv.at[j, k, c], {"group": g})
+                    copy.start()
+                    copies.append(copy)
+                pass_on(j, 0, c, at)
+        origins = [lax.rem(group + groups - k - 1, groups) for k in range(groups - 1)]
+        for c in range(chunks):
+            for j in range(others):
+                for k, origin in enumerate(origins):
+                    at = place(lax.rem(me + count - 2 * (j + 1), count), origin, c)
+                    remote(at, at, across_send.at[j, k, c], across_recv.at[j, k, c],
+                           {"group": rest[k]}).wait_recv()
+                    pass_on(j, k + 1, c, at)
+        at = o_ref.at[span(mate, rows)]
+        remote(at, at, own_send, own_recv, {"head": mate}).wait_recv()
+        for c in range(chunks):
+            for j in range(others):
+                for k, origin in enumerate([group] + origins):
+                    at = place(lax.rem(mate + count - 2 * (j + 1), count), origin, c)
+                    remote(at, at, on_send.at[j, k, c], on_recv.at[j, k, c],
+                           {"head": mate}).wait_recv()
+        own.wait_send()
+        for copy in copies:
+            copy.wait_send()
+
+    dma = pltpu.SemaphoreType.DMA
+    far_sem = dma((max(others, 1), chunks))
+    across = dma((max(others, 1), max(groups - 1, 1), chunks))
+    on = dma((max(others, 1), groups, chunks))
+    return comm_call(
+        kernel, jax.ShapeDtypeStruct((count * rows, width), block.dtype),
+        [far_sem, far_sem, dma, dma, across, across, on, on], collective_id, block,
+    )
+
+
 def sum_to_rows(partial, collective_id):
     count, groups = lax.axis_size("head"), lax.axis_size("group")
     rows, width = partial.shape[0] // count, partial.shape[1]
-    chunks = 4
+    chunks = 8
     part = rows // chunks
     pairs = count // 2
 
@@ -353,17 +429,23 @@
         for j in range(lay.groups - 1):
             self.crossing(0, j, me, group).start()
 
-    def finish(self):
+    def forward(self, part=0, parts=1):
         lay = self.layout
         me, group = lay.here(), lax.axis_index("group")
-
-        @pl.loop(1, lay.owners)
+        begin = 1 + part * (lay.owners - 1) // parts
+        end = 1 + (part + 1) * (lay.owners - 1) // parts
+
+        @pl.loop(begin, end)
         def _(k):
             source = lax.rem(me + lay.owners - k, lay.owners)
             place = self.landed.at[group, span(source, lay.slab)]
             remote(place, place, self.over_send.at[k], self.over_recv.at[k], lay.peer(source)).wait_recv()
             for j in range(lay.groups - 1):
                 self.crossing(k, j, source, group).start()
+
+    def finish(self):
+        lay = self.layout
+        me, group = lay.here(), lax.axis_index("group")
 
         @pl.loop(0, lay.owners)
         def _(k):
@@ -401,6 +483,7 @@
         routed.bind(refs[: routed.inputs], refs[routed.inputs], refs[routed.inputs + 1 :])
         routed.greet()
         routed.start()
+        routed.forward()
         routed.finish()
 
     return comm_call(kernel, routed.out, routed.scratch, collective_id, *routed.operands)
@@ -570,8 +653,8 @@
     grad_normed = route_back(lay, returned, takes, 3).astype(jnp.float32)
     grad_hidden = grad_f + norm_backward(hidden_f, scale_two, gain_ffn, grad_normed)
     grad_hidden_b = grad_hidden.astype(jnp.bfloat16)
-    shard_rows = gather_head(grad_hidden_b, 4)
-    weight_total = jnp.einsum("rh,rd->hd", mixed, shard_rows, preferred_element_type=jnp.float32)
+    shard_rows = gather_head_split(grad_hidden_b, 4)
+    weight_total = jnp.einsum("rh,rd->dh", mixed, shard_rows, preferred_element_type=jnp.float32)
     fresh = jnp.einsum(
         "rd,hd->rh", shard_rows, w_attn_out, preferred_element_type=jnp.float32
     ).astype(jnp.bfloat16)
@@ -600,14 +683,12 @@
         ),
         5,
     )
-    grad_proj_sum, grad_out_sum = (
-        lax.psum_scatter(
-            grad_proj.astype(jnp.bfloat16), "dp", scatter_dimension=1, tiled=True
-        ).astype(jnp.float32),
-        lax.psum_scatter(
-            grad_out_w.astype(jnp.bfloat16), "dp", scatter_dimension=1, tiled=True
-        ).astype(jnp.float32),
-    )
+    weight_grads = jnp.concatenate(
+        [grad_proj.astype(jnp.bfloat16), grad_out_w.astype(jnp.bfloat16)[None]], axis=0
+    )
+    summed = lax.psum_scatter(weight_grads, "dp", scatter_dimension=1, tiled=True)
+    grad_proj_sum = summed[:-1].astype(jnp.float32)
+    grad_out_sum = summed[-1].T.astype(jnp.float32)
     grad_tokens = (
         grad_hidden + norm_backward(tokens_f, scale_one, gain_attn, grad_normed_one)
     ).astype(jnp.bfloat16)

time: 243 us -> 231 us (0.951)
  Pallas kernels: 165 us -> 153 us
  other arithmetic: 14.9 us -> 18.4 us
  waiting for transfers between devices: 11.6 us -> 8.33 us
    pallas_call x6, Pallas kernels: 165 us -> 153 us  [comm_call(): pl.pallas_call(kernel, out_shape=out, in_specs=[pl.BlockSpec(memory_space...]
    reduce_scatter x2 -> x1, waiting for transfers between devices: 11.6 us -> 8.32 us  [body(): lax.psum_scatter(weight_grads, 'dp', scatter_dimension=1, tiled=True)]
    unnamed x86 -> x68, local copies, waits for them, and re-layouts: 7.35 us -> 6.37 us
  transfers between devices with their start and end apart: 2 -> 1, of which waited for: 1 -> 1; matrix products, arithmetic and copies ran while one was open for 9% -> 6% of each run, Pallas kernels for 9% -> 9%
where the time goes in v3:
time: 231 us
  Pallas kernels  153 us (66%)
  matrix products  28.5 us (12%)
  other arithmetic  18.4 us (8%)
  between operations  14.7 us (6%)
  waiting for transfers between devices  8.33 us (4%)
  local copies, waits for them, and re-layouts  7.26 us (3%)
    pallas_call x6, Pallas kernels, comm_call(): pl.pallas_call(kernel, out_shape=out, in_specs=[pl.BlockSpec(memory_space...  153 us
    reduce_scatter x1, waiting for transfers between devices, body(): lax.psum_scatter(weight_grads, 'dp', scatter_dimension=1, tiled=True)  8.32 us
    unnamed x68, local copies, waits for them, and re-layouts  6.37 us
  transfers between devices with their start and end apart: 1, of which 1 were waited for; matrix products, arithmetic and copies ran while one was open for 6% of the time, Pallas kernels for 9%

profile of v3, /device:TPU:0, one launch (start us, length us, event | category | flops | bytes accessed | tf_op | source)
XLA Modules:
  0.0 230.6 jit_solution(9924546788391615391)
XLA Ops:
  7.3 0.9 copy.44
  8.5 0.6 reduce-window.6
  9.6 0.8 multiply_add_fusion
  10.8 1.2 fusion.58
  12.1 1.1 fusion.35
  13.4 1.2 fusion.52.refs_0_
  14.7 1.0 and_convert_fusion.1.refs_2_.refs_1_
  15.7 35.8 %shard_map.155 = (bf16[512,2048]{1,0:T(8,128)(2,1)}, bf16[320,2048]{1,0:T(8,128)(2,1)S(1)}) custom-call(bf16[128,2048]{1,0:T(8,128)(2,1)S(1)} %fusion.52.refs_0_, bf16[128,2048]{1,0:T(8,128)(2,1)S(1)} %copy-done.1, bf16[4,1280,128]{2,1,0:T(8,128)(2,1)S(1)} %and_convert_fusion.1.refs_2_.refs_1_, bf16[4,80,320]{2,1,0:T(8,128)(2,1)S(1)} %copy-done.6, ...), custom_call_target="tpu_custom_call" | custom-call | tf_op jit(solution)/shard_map/pallas_call | solution.py:91
  51.6 3.3 %fusion.39 = bf16[3,512,128]{2,1,0:T(8,128)(2,1)S(1)} fusion(bf16[3,2048,128]{2,1,0:T(8,128)(2,1)S(1)} %copy-done.21, bf16[512,2048]{1,0:T(8,128)(2,1)} %get-tuple-element.7), kind=kOutput, calls=%fused_computation.53 | convolution fusion | flops 805502976 | bytes 4063232 | tf_op jit(solution)/shard_map/rd,idh->irh/dot_general | solution.py:618
  54.9 0.3 fusion.87
  55.4 0.3 fusion.42
  55.7 0.7 copy-done.14
  56.4 0.7 convolution_convert_fusion.3.p_ref
  57.2 18.8 %shard_map.156 = f32[128,2048]{1,0:T(8,128)S(1)} custom-call(bf16[512,2048]{1,0:T(8,128)(2,1)S(1)} %convolution_convert_fusion.3.p_ref), custom_call_target="tpu_custom_call" | custom-call | tf_op jit(solution)/shard_map/pallas_call | solution.py:91
  76.5 29.9 %shard_map.157 = bf16[320,2048]{1,0:T(8,128)(2,1)S(1)} custom-call(bf16[128,2048]{1,0:T(8,128)(2,1)S(1)} %fusion.46.refs_0_, bf16[4,1280,128]{2,1,0:T(8,128)(2,1)S(1)} %and_convert_fusion.1.refs_2_.refs_1_, bf16[4,80,320]{2,1,0:T(8,128)(2,1)S(1)} %copy-done.6), custom_call_target="tpu_custom_call" | custom-call | tf_op jit(solution)/shard_map/pallas_call | solution.py:91
  106.4 3.5 %fusion.5 = f32[320,704]{1,0:T(8,128)S(1)} fusion(bf16[320,2048]{1,0:T(8,128)(2,1)S(1)} %shard_map.157, bf16[1,2,2048,704]{2,3,1,0:T(8,128)(2,1)} %param.18), kind=kOutput, calls=%fused_computation.11 | convolution fusion | flops 922746880 | bytes 5095424 | tf_op jit(solution)/shard_map/esd,edf->esf/dot_general | solution.py:46
  110.0 3.4 %fusion.9 = f32[320,704]{1,0:T(8,128)S(1)} fusion(bf16[320,2048]{1,0:T(8,128)(2,1)S(1)} %shard_map.157, bf16[1,2,2048,704]{2,3,1,0:T(8,128)(2,1)} %param.18), kind=kOutput, calls=%fused_computation.15 | convolution fusion | flops 922746880 | bytes 5095424 | tf_op jit(solution)/shard_map/esd,edf->esf/dot_general | solution.py:47
  113.4 0.3 and_convert_fusion.take_ref
  113.7 1.4 multiply_convert_fusion.2
  115.2 0.7 slice-done
  115.9 0.8 slice-done.1
  116.8 1.2 fusion.3
  118.0 1.2 fusion.16.p_ref
  119.3 36.1 %shard_map.158 = bf16[128,2048]{1,0:T(8,128)(2,1)S(1)} custom-call(bf16[320,2048]{1,0:T(8,128)(2,1)S(1)} %fusion.16.p_ref, bf16[4,320,80]{2,1,0:T(8,128)(2,1)S(1)} %copy-done.7, bf16[4,128,1280]{2,1,0:T(8,128)(2,1)S(1)} %and_convert_fusion.take_ref), custom_call_target="tpu_custom_call" | custom-call | tf_op jit(solution)/shard_map/pallas_call | solution.py:91
  155.4 0.3 fusion.47
  155.8 0.4 fusion.67.x_ref
  156.2 12.8 %shard_map.159 = bf16[512,2048]{1,0:T(8,128)(2,1)S(1)} custom-call(bf16[128,2048]{1,0:T(8,128)(2,1)S(1)} %fusion.67.x_ref), custom_call_target="tpu_custom_call" | custom-call | tf_op jit(solution)/shard_map/pallas_call | solution.py:91
  169.0 0.7 convolution_convert_fusion.9
  169.7 0.4 fusion.24
  170.2 0.3 fusion.45
  170.5 0.3 multiply_reduce_fusion
  170.9 0.3 multiply_convert_fusion
  171.1 0.3 fusion.44
  171.7 0.7 copy-done.20
  172.4 1.0 fusion.19
  173.4 1.5 pad_maximum_fusion.1
  175.0 2.9 %bitcast_convert_fusion.p_ref = bf16[512,2048]{1,0:T(8,128)(2,1)S(1)} fusion(bf16[3,2048,128]{2,1,0:T(8,128)(2,1)} %param.14, bf16[1,512,1,128]{1,3,2,0:T(8,128)(2,1)} %copy-done.22, bf16[1,512,1,128]{1,3,2,0:T(8,128)(2,1)S(1)} %fusion.44, bf16[1,512,1,128]{1,3,2,0:T(8,128)(2,1)} %copy-done.16), kind=kOutput, calls=%fused_computation.1 | convolution fusion | flops 806748160 | bytes 4063232 | tf_op jit(solution)/shard_map/irh,idh->rd/dot_general | solution.py:681
  177.9 19.9 %shard_map.160 = f32[128,2048]{1,0:T(8,128)S(1)} custom-call(bf16[512,2048]{1,0:T(8,128)(2,1)S(1)} %bitcast_convert_fusion.p_ref), custom_call_target="tpu_custom_call" | custom-call | tf_op jit(solution)/shard_map/pallas_call | solution.py:91
  197.8 0.3 fusion.53
  198.2 1.7 fusion.1
  199.9 1.7 fusion
  201.7 3.0 %pad_maximum_fusion = bf16[1,2,2048,704]{2,3,1,0:T(8,128)(2,1)} fusion(bf16[1,1,2048,704]{2,3,1,0:T(8,128)(2,1)S(1)} %fusion.1, bf16[1,1,2048,704]{2,3,1,0:T(8,128)(2,1)S(1)} %fusion), kind=kLoop, calls=%fused_computation | loop fusion | flops 2883584 | bytes 11534336 | tf_op jit(solution)/shard_map/stack | solution.py:57
  204.7 3.3 %fusion.2 = bf16[1,704,2048]{2,1,0:T(8,128)(2,1)} fusion(bf16[320,2048]{1,0:T(8,128)(2,1)S(1)} %copy-done.9, f32[320,704]{1,0:T(8,128)S(1)} %copy-done.30, f32[320,704]{1,0:T(8,128)S(1)} %copy-done.28), kind=kOutput, calls=%fused_computation.8 | convolution fusion | flops 925540352 | bytes 5996544 | tf_op jit(solution)/shard_map/esf,esd->efd/dot_general | solution.py:52
  208.1 1.4 fusion.57
  209.5 8.3 %reduce-scatter.2.cloned.1.call-done = bf16[4,512,128]{1,2,0:T(8,128)(2,1)} async-done(((bf16[4,2048,128]{1,2,0:T(8,128)(2,1)}), bf16[4,512,128]{1,2,0:T(8,128)(2,1)}) %reduce-scatter.2.cloned.1.call-update) | async-done | bytes 524304 | tf_op jit(solution)/shard_map/reduce_scatter | solution.py:689
  217.8 2.0 slice_convert_fusion
  219.8 2.3 copy.51
  222.1 1.6 convert_bitcast_fusion
  (88 shorter events, 2.6 us)
Async XLA Ops:
  7.2 106.5 %copy-start = (bf16[1,704,2048]{2,1,0:T(8,128)(2,1)S(1)}, bf16[1,704,2048]{2,1,0:T(8,128)(2,1)}, u32[]{:S(2)}) copy-start(bf16[1,704,2048]{2,1,0:T(8,128)(2,1)} %param.19) | copy-start | bytes 8650756
  7.2 210.7 %reduce-scatter.2.cloned.1.call-start = ((), (), s32[]{:S(2)}) async-start(), calls=%async_computation.1 | async-start | bytes 2621440 | tf_op jit(solution)/shard_map/reduce_scatter | solution.py:689
  9.6 6.2 %copy-start.1 = (bf16[128,2048]{1,0:T(8,128)(2,1)S(1)}, bf16[128,2048]{1,0:T(8,128)(2,1)}, u32[]{:S(2)}) copy-start(bf16[128,2048]{1,0:T(8,128)(2,1)} %refs_1_.1) | copy-start | bytes 1572868
  9.6 6.1 %copy-start.6 = (bf16[4,80,320]{2,1,0:T(8,128)(2,1)S(1)}, bf16[4,80,320]{2,1,0:T(8,128)(2,1)}, u32[]{:S(2)}) copy-start(bf16[4,80,320]{2,1,0:T(8,128)(2,1)} %constant.80.clone.refs_3_.refs_2_) | copy-start | bytes 614404
  14.7 36.9 %copy-start.21 = (bf16[3,2048,128]{2,1,0:T(8,128)(2,1)S(1)}, bf16[3,2048,128]{2,1,0:T(8,128)(2,1)}, u32[]{:S(2)}) copy-start(bf16[3,2048,128]{2,1,0:T(8,128)(2,1)} %param.14) | copy-start | bytes 4718596
  51.5 62.1 %copy-start.8 = (bf16[320,2048]{1,0:T(8,128)(2,1)}, bf16[320,2048]{1,0:T(8,128)(2,1)S(1)}, u32[]{:S(2)}) copy-start(bf16[320,2048]{1,0:T(8,128)(2,1)S(1)} %get-tuple-element.8) | copy-start | bytes 3932164
  55.4 1.0 copy-start.14
  57.2 18.9 %copy-start.10 = (bf16[128,2048]{1,0:T(8,128)(2,1)S(1)}, bf16[128,2048]{1,0:T(8,128)(2,1)}, u32[]{:S(2)}) copy-start(bf16[128,2048]{1,0:T(8,128)(2,1)} %param.12) | copy-start | bytes 1572868
  57.2 19.1 %copy-start.15 = (f32[2048]{0:T(1024)S(1)}, f32[2048]{0:T(1024)}, u32[]{:S(2)}) copy-start(f32[2048]{0:T(1024)} %param.17) | copy-start | bytes 24580
  76.3 79.5 %copy-start.12 = (bf16[128,2048]{1,0:T(8,128)(2,1)}, bf16[128,2048]{1,0:T(8,128)(2,1)S(1)}, u32[]{:S(2)}) copy-start(bf16[128,2048]{1,0:T(8,128)(2,1)S(1)} %get-tuple-element.30) | copy-start | bytes 1572868
  106.4 3.5 %copy-start.4 = (bf16[320,2048]{1,0:T(8,128)(2,1)}, bf16[320,2048]{1,0:T(8,128)(2,1)S(1)}, u32[]{:S(2)}) copy-start(bf16[320,2048]{1,0:T(8,128)(2,1)S(1)} %shard_map.157) | copy-start | bytes 3932164
  110.0 3.7 %copy-start.27 = (f32[320,704]{1,0:T(8,128)}, f32[320,704]{1,0:T(8,128)S(1)}, u32[]{:S(2)}) copy-start(f32[320,704]{1,0:T(8,128)S(1)} %fusion.5) | copy-start | bytes 2703364
  113.4 1.8 copy-start.29
  113.4 2.5 %slice-start = ((s8[5767168]{0:T(1024)(128)(4,1)}), s8[4194304]{0:T(1024)(128)(4,1)S(1)}, s32[]{:S(2)}) async-start(s8[5767168]{0:T(1024)(128)(4,1)} %bitcast.136), calls=%async_computation.2 | async-start | bytes 8388608
  113.7 3.1 %slice-start.1 = ((s8[5767168]{0:T(1024)(128)(4,1)}), s8[1572864]{0:T(1024)(128)(4,1)S(1)}, s32[]{:S(2)}) async-start(s8[5767168]{0:T(1024)(128)(4,1)} %bitcast.136), calls=%async_computation.3 | async-start | bytes 3145728
  115.2 2.8 %copy-start.23 = (bf16[320,704]{1,0:T(8,128)(2,1)}, bf16[320,704]{1,0:T(8,128)(2,1)S(1)}, u32[]{:S(2)}) copy-start(bf16[320,704]{1,0:T(8,128)(2,1)S(1)} %get-tuple-element.32) | copy-start | bytes 1351684
  115.2 2.8 %copy-start.25 = (bf16[320,704]{1,0:T(8,128)(2,1)}, bf16[320,704]{1,0:T(8,128)(2,1)S(1)}, u32[]{:S(2)}) copy-start(bf16[320,704]{1,0:T(8,128)(2,1)S(1)} %get-tuple-element.31) | copy-start | bytes 1351684
  118.0 1.3 copy-start.7
  119.3 36.5 %copy-start.2 = (bf16[128,2048]{1,0:T(8,128)(2,1)S(1)}, bf16[128,2048]{1,0:T(8,128)(2,1)}, u32[]{:S(2)}) copy-start(bf16[128,2048]{1,0:T(8,128)(2,1)} %refs_1_.1) | copy-start | bytes 1572868
  155.8 13.2 %copy-start.18 = (f32[128]{0:T(128)}, f32[128]{0:T(128)S(1)}, u32[]{:S(2)}) copy-start(f32[128]{0:T(128)S(1)} %broadcast_multiply_fusion.1) | copy-start | bytes 1540
  170.5 1.2 copy-start.22
  170.8 1.6 copy-start.20
  172.4 1.0 copy-start.16
  177.9 19.9 %copy-start.11 = (bf16[128,2048]{1,0:T(8,128)(2,1)S(1)}, bf16[128,2048]{1,0:T(8,128)(2,1)}, u32[]{:S(2)}) copy-start(bf16[128,2048]{1,0:T(8,128)(2,1)} %param.12) | copy-start | bytes 1572868
  177.9 19.9 %copy-start.17 = (f32[2048]{0:T(1024)S(1)}, f32[2048]{0:T(1024)}, u32[]{:S(2)}) copy-start(f32[2048]{0:T(1024)} %param.16) | copy-start | bytes 24580
  177.9 20.3 %copy-start.5 = (bf16[320,2048]{1,0:T(8,128)(2,1)S(1)}, bf16[320,2048]{1,0:T(8,128)(2,1)}, u32[]{:S(2)}) copy-start(bf16[320,2048]{1,0:T(8,128)(2,1)} %copy-done.4) | copy-start | bytes 3932164
  177.9 20.3 %copy-start.26 = (bf16[320,704]{1,0:T(8,128)(2,1)S(1)}, bf16[320,704]{1,0:T(8,128)(2,1)}, u32[]{:S(2)}) copy-start(bf16[320,704]{1,0:T(8,128)(2,1)} %copy-done.25) | copy-start | bytes 1351684
  198.2 1.7 copy-start.24
  201.6 3.1 %copy-start.9 = (bf16[320,2048]{1,0:T(8,128)(2,1)S(1)}, bf16[320,2048]{1,0:T(8,128)(2,1)}, u32[]{:S(2)}) copy-start(bf16[320,2048]{1,0:T(8,128)(2,1)} %copy-done.8) | copy-start | bytes 3932164
  201.6 3.1 %copy-start.28 = (f32[320,704]{1,0:T(8,128)S(1)}, f32[320,704]{1,0:T(8,128)}, u32[]{:S(2)}) copy-start(f32[320,704]{1,0:T(8,128)} %copy-done.27) | copy-start | bytes 2703364
  201.7 3.0 %copy-start.30 = (f32[320,704]{1,0:T(8,128)S(1)}, f32[320,704]{1,0:T(8,128)}, u32[]{:S(2)}) copy-start(f32[320,704]{1,0:T(8,128)} %copy-done.29) | copy-start | bytes 2703364
  204.7 3.4 %copy-start.3 = (bf16[128,2048]{1,0:T(8,128)(2,1)S(1)}, bf16[128,2048]{1,0:T(8,128)(2,1)}, u32[]{:S(2)}) copy-start(bf16[128,2048]{1,0:T(8,128)(2,1)} %refs_1_.1) | copy-start | bytes 1572868
  204.7 3.4 %copy-start.13 = (bf16[128,2048]{1,0:T(8,128)(2,1)S(1)}, bf16[128,2048]{1,0:T(8,128)(2,1)}, u32[]{:S(2)}) copy-start(bf16[128,2048]{1,0:T(8,128)(2,1)} %copy-done.12) | copy-start | bytes 1572868
  204.7 3.4 %copy-start.19 = (f32[128]{0:T(128)S(1)}, f32[128]{0:T(128)}, u32[]{:S(2)}) copy-start(f32[128]{0:T(128)} %copy-done.18) | copy-start | bytes 1540
Sparse Core Ops, SparseCore 0:
  175.1 42.6 reduce-scatter.1
